TPU v7x, 256 devices: a whole 4x4x8 slice. The times are simulated.
256 devices in a mesh: dp: 32 (over z, x), ep: 8 (over y, core).
Axes of the slice: x: 4, y: 4, z: 8, core: 2. Of those that a mesh axis runs over, the one named last changes fastest.
Arguments:
- drafts_in: bfloat16 [512, 7168], P('dp'), may hold values from -6 to 6
- cache: bfloat16 [512, 1024, 576], P(('dp', 'ep')), may hold values from -8 to 8
- queries: bfloat16 [4, 512, 64, 576], P(None, ('dp', 'ep')), may hold values from -40 to 40
- lengths: int32 [512], P(('dp', 'ep')), may hold values from 256 to 1024, as said below
- counts: int32 [32], P('dp'), may hold values from 1 to 16, as said below
- routes: int32 [4, 512, 8], P(None, 'dp'), may hold values from 0 to 31, all different within a row; in each aligned block of 16 rows (0 to 15, 16 to 31, ..., all dimensions but the last counted through in order) at most 4 rows name the same one
- norm_gain: float32 [7168], replicated, may hold values from 0.5 to 1.5
- kv_weight: bfloat16 [7168, 576], P('ep'), may hold values from -0.0625 to 0.0625
- kv_gain: float32 [512], replicated, may hold values from 0.5 to 1.5
- router: bfloat16 [7168, 32], replicated, may hold values from -0.0625 to 0.0625
- w_gate: bfloat16 [32, 7168, 1024], P('dp', None, 'ep'), may hold values from -0.0625 to 0.0625
- w_up: bfloat16 [32, 7168, 1024], P('dp', None, 'ep'), may hold values from -0.0625 to 0.0625
- w_down: bfloat16 [32, 1024, 7168], P('dp', 'ep'), may hold values from -0.1875 to 0.1875
Outputs:
- drafted: bfloat16 [4, 512, 7168], P(None, 'dp', 'ep')
- attended: bfloat16 [4, 512, 64, 512], P(None, ('dp', 'ep'))
Inputs may be any that keep to these rules, and one draw needn't show every extreme that they name: `lengths`: some request slot of every draw has all 1024 positions in use. `counts`: some rank has all 16 slots live in every draw. `routes`: each row names 8 different experts; among the 16 rows of one rank at one step, at most 4 name the same expert.
All inputs are finite; a program needn't handle non-finite values.
Results may differ from a plain program's by a relative error of at most 0.025.
Values may be sent and summed in bfloat16 or wider, within the bound.
A program may use at most 128 MiB of HBM per device.

v0:
```python
import jax
import jax.numpy as jnp
from jax import lax
from jax.sharding import PartitionSpec as P

LAT = 512
TOP = 8
STEPS = 4


SCALE = 0.07216878364870322
ROUTE_SCALE = 2.827
EPSILON = 1e-06
THETA = 50000.0
NEGATIVE = -1e30


def normalize(values):
    return values * lax.rsqrt(jnp.mean(values * values, axis=-1, keepdims=True) + EPSILON)


def rounded(values):
    return lax.optimization_barrier(values.astype(jnp.bfloat16)).astype(jnp.float32)


def rotate(values, position):
    middle = values.shape[-1] // 2
    frequency = THETA ** (-jnp.arange(middle, dtype=jnp.float32) / middle)
    angles = position.astype(jnp.float32)[:, None] * frequency[None, :]
    former = values[:, :middle]
    latter = values[:, middle:]
    cosine = jnp.cos(angles)
    sine_part = jnp.sin(angles)
    return jnp.concatenate(
        [former * cosine - latter * sine_part, former * sine_part + latter * cosine], axis=-1
    )


def make_key(latent_raw, kv_gain, position):
    latent = normalize(latent_raw[:, :LAT]) * kv_gain
    turned = rotate(latent_raw[:, LAT:], position)
    return jnp.concatenate([latent, turned], axis=-1).astype(jnp.bfloat16)


def shards(
    drafts_in,
    cache,
    queries,
    lengths,
    counts,
    routes,
    norm_gain,
    kv_weight,
    kv_gain,
    router,
    w_gate,
    w_up,
    w_down,
):
    member = lax.axis_index("ep")
    groups = lax.axis_size("ep")
    slot_count, model_width = drafts_in.shape
    feature_share = model_width // groups
    per_device = lengths.shape[0]
    experts = router.shape[1]
    local_experts = w_gate.shape[0]
    rank_count = experts // local_experts
    capacity = max(2, slot_count * TOP // experts)
    active = jnp.arange(slot_count) < counts[0]
    own_active = member * per_device + jnp.arange(per_device) < counts[0]
    cache_valid = jnp.arange(cache.shape[1])[None, :] < lengths[:, None]
    hidden_state = drafts_in
    keys_list = []
    attended = []
    drafted = []
    for step_index in range(STEPS):
        hidden_wide = hidden_state.astype(jnp.float32)
        normed = (normalize(hidden_wide) * norm_gain).astype(jnp.bfloat16)
        own_columns = lax.dynamic_slice_in_dim(normed, member * feature_share, feature_share, 1)
        latent_raw = lax.psum_scatter(
            jnp.dot(own_columns, kv_weight, preferred_element_type=jnp.float32).astype(
                jnp.bfloat16
            ),
            "ep",
            scatter_dimension=0,
            tiled=True,
        ).astype(jnp.float32)
        keys_list.append(make_key(latent_raw, kv_gain, lengths + step_index))
        draft_keys = jnp.stack(keys_list, axis=1)
        query_now = queries[step_index]
        cache_scores = SCALE * jnp.einsum(
            "thk,tpk->thp", query_now, cache, preferred_element_type=jnp.float32
        )
        cache_scores = jnp.where(cache_valid[:, None, :], cache_scores, NEGATIVE)
        draft_scores = SCALE * jnp.einsum(
            "thk,tjk->thj", query_now, draft_keys, preferred_element_type=jnp.float32
        )
        highest = jnp.maximum(jnp.max(cache_scores, axis=-1), jnp.max(draft_scores, axis=-1))
        cache_weight = jnp.where(
            cache_valid[:, None, :], jnp.exp(cache_scores - highest[..., None]), 0.0
        )
        draft_weight = jnp.exp(draft_scores - highest[..., None])
        numerator = jnp.einsum(
            "thp,tpl->thl",
            cache_weight.astype(jnp.bfloat16),
            cache[:, :, :LAT],
            preferred_element_type=jnp.float32,
        )
        numerator = numerator + jnp.einsum(
            "thj,tjl->thl",
            draft_weight.astype(jnp.bfloat16),
            draft_keys[:, :, :LAT],
            preferred_element_type=jnp.float32,
        )
        denominator = jnp.sum(cache_weight, axis=-1) + jnp.sum(draft_weight, axis=-1)
        attention_out = numerator / denominator[..., None]
        attended.append(
            jnp.where(own_active[:, None, None], attention_out, 0.0).astype(jnp.bfloat16)
        )
        gate_scores = jax.nn.sigmoid(jnp.dot(normed, router, preferred_element_type=jnp.float32))
        picked = routes[step_index]
        matches = picked[:, :, None] == jnp.arange(experts)[None, None, :]
        chosen = jnp.sum(jnp.where(matches, gate_scores[:, None, :], 0.0), axis=-1)
        weights = chosen / jnp.sum(chosen, axis=1, keepdims=True) * ROUTE_SCALE
        flattened = (
            (matches & active[:, None, None]).astype(jnp.int32).reshape(slot_count * TOP, experts)
        )
        earlier = jnp.cumsum(flattened, axis=0) - flattened
        slot_of = jnp.sum(earlier * flattened, axis=-1).reshape(slot_count, TOP)
        target = picked * capacity + slot_of
        placed = (target[:, :, None] == jnp.arange(experts * capacity)[None, None, :]) & active[
            :, None, None
        ]
        dispatch_table = jnp.any(placed, axis=1).astype(jnp.bfloat16)
        combine_table = jnp.sum(jnp.where(placed, weights[:, :, None], 0.0), axis=1)
        outgoing = jnp.einsum(
            "tr,td->rd", dispatch_table, normed, preferred_element_type=jnp.float32
        ).astype(jnp.bfloat16)
        outgoing = outgoing.reshape(rank_count, local_experts, capacity, model_width)
        received = lax.all_to_all(outgoing, "dp", split_axis=0, concat_axis=0, tiled=True)
        gate_value = jnp.einsum(
            "sekd,edf->sekf", received, w_gate, preferred_element_type=jnp.float32
        )
        up_value = jnp.einsum("sekd,edf->sekf", received, w_up, preferred_element_type=jnp.float32)
        hidden_units = (jax.nn.silu(gate_value) * up_value).astype(jnp.bfloat16)
        partial_value = jnp.einsum(
            "sekf,efd->sekd", hidden_units, w_down, preferred_element_type=jnp.float32
        )
        summed = lax.psum_scatter(
            rounded(partial_value).astype(jnp.bfloat16), "ep", scatter_dimension=3, tiled=True
        )
        returned = lax.all_to_all(summed, "dp", split_axis=0, concat_axis=0, tiled=True)
        returned = returned.reshape(experts * capacity, feature_share).astype(jnp.float32)
        update = jnp.dot(combine_table, returned, precision=lax.Precision.HIGHEST)
        own_hidden = lax.dynamic_slice_in_dim(hidden_wide, member * feature_share, feature_share, 1)
        new_slice = (own_hidden + update).astype(jnp.bfloat16)
        drafted.append(jnp.where(active[:, None], new_slice, 0.0))
        if step_index + 1 < STEPS:
            hidden_state = lax.all_gather(new_slice, "ep", axis=1, tiled=True)
    return (jnp.stack(drafted), jnp.stack(attended))


def solution(mesh):
    return jax.shard_map(
        shards,
        mesh=mesh,
        in_specs=(
            P("dp", None),
            P(("dp", "ep"), None, None),
            P(None, ("dp", "ep"), None, None),
            P(("dp", "ep")),
            P("dp"),
            P(None, "dp", None),
            P(),
            P("ep", None),
            P(),
            P(),
            P("dp", None, "ep"),
            P("dp", None, "ep"),
            P("dp", "ep", None),
        ),
        out_specs=(P(None, "dp", "ep"), P(None, ("dp", "ep"), None, None)),
        check_vma=False,
    )
```

profile of v0, /device:TPU:32, one launch (start us, length us, event | category | flops | bytes accessed | tf_op | source)
XLA Modules:
  0.0 664.1 jit_solution(2607924721375177943)
XLA Ops:
  22.0 56.3 %all_to_all.40 = bf16[32,1,4,7168]{3,2,1,0:T(4,128)(2,1)S(1)} all-to-all(bf16[32,1,4,7168]{3,2,1,0:T(4,128)(2,1)} %bitcast.416), channel_id=1, replica_groups=mesh['dp'=32,'ep'=8] {'dp'}, dimensions={0} | all-to-all | bytes 3670016 | tf_op jit(solution)/shard_map/all_to_all | solution.py:140
  80.5 4.9 fusion
  85.4 9.7 %copy.317 = bf16[32,1,4,7168]{0,2,1,3:T(4,128)(2,1)} copy(bf16[32,1,4,7168]{3,0,2,1:T(8,128)(2,1)} %fusion) | data formatting | bytes 3670016
  95.1 9.5 %reshape.613 = bf16[7168,128]{1,0:T(8,128)(2,1)} reshape(bf16[7168,1,4,32]{3,2,1,0:T(4,128)(2,1)} %bitcast.411) | data formatting | bytes 3670016
  106.7 30.7 %reduce-scatter.13.cloned.1.call-done = bf16[896,128]{1,0:T(8,128)(2,1)} async-done(((bf16[7168,128]{1,0:T(8,128)(2,1)}), bf16[896,128]{1,0:T(8,128)(2,1)}) %reduce-scatter.13.cloned.1.call-update) | async-done | bytes 229392
  141.0 10.1 %all-to-all-start.1 = ((bf16[32,1,4,896]{3,2,1,0:T(4,128)(2,1)}), bf16[32,1,4,896]{3,2,1,0:T(4,128)(2,1)S(1)}, u32[]{:S(2)}, u32[]{:S(2)}) async-start(bf16[32,1,4,896]{3,2,1,0:T(4,128)(2,1)} %copy.280), calls=%async_computation.1 | async-start | bytes 458752 | tf_op jit(solution)/shard_map/all_to_all | solution.py:152
  151.6 9.9 %all-to-all-done.1 = bf16[32,1,4,896]{3,2,1,0:T(4,128)(2,1)S(1)} async-done(((bf16[32,1,4,896]{3,2,1,0:T(4,128)(2,1)}), bf16[32,1,4,896]{3,2,1,0:T(4,128)(2,1)S(1)}, u32[]{:S(2)}, u32[]{:S(2)}) %all-to-all-start.1) | async-done | bytes 229408 | tf_op jit(solution)/shard_map/all_to_all | solution.py:152
  162.7 12.8 %all_gather.9 = bf16[16,7168]{1,0:T(8,128)(2,1)S(1)} all-gather(bf16[16,896]{1,0:T(8,128)(2,1)S(1)} %fusion.192), channel_id=1, replica_groups=mesh['dp'=32,'ep'=8] {'ep'}, dimensions={1}, use_global_device_ids=true | all-gather | bytes 258048 | tf_op jit(solution)/shard_map/all_gather | solution.py:159
  181.8 49.9 %all_to_all.41 = bf16[32,1,4,7168]{3,2,1,0:T(4,128)(2,1)S(1)} all-to-all(bf16[32,1,4,7168]{3,2,1,0:T(4,128)(2,1)} %bitcast.417), channel_id=1, replica_groups=mesh['dp'=32,'ep'=8] {'dp'}, dimensions={0} | all-to-all | bytes 3670016 | tf_op jit(solution)/shard_map/all_to_all | solution.py:140
  233.9 4.9 fusion.1
  238.8 9.7 %copy.319 = bf16[32,1,4,7168]{0,2,1,3:T(4,128)(2,1)} copy(bf16[32,1,4,7168]{3,0,2,1:T(8,128)(2,1)} %fusion.1) | data formatting | bytes 3670016
  248.5 9.5 %reshape.615 = bf16[7168,128]{1,0:T(8,128)(2,1)} reshape(bf16[7168,1,4,32]{3,2,1,0:T(4,128)(2,1)} %bitcast.412) | data formatting | bytes 3670016
  259.2 30.8 %reduce-scatter.15.cloned.1.call-done = bf16[896,128]{1,0:T(8,128)(2,1)} async-done(((bf16[7168,128]{1,0:T(8,128)(2,1)}), bf16[896,128]{1,0:T(8,128)(2,1)}) %reduce-scatter.15.cloned.1.call-update) | async-done | bytes 229392
  293.6 10.1 %all-to-all-start.3 = ((bf16[32,1,4,896]{3,2,1,0:T(4,128)(2,1)}), bf16[32,1,4,896]{3,2,1,0:T(4,128)(2,1)S(1)}, u32[]{:S(2)}, u32[]{:S(2)}) async-start(bf16[32,1,4,896]{3,2,1,0:T(4,128)(2,1)} %copy.287), calls=%async_computation.3 | async-start | bytes 458752 | tf_op jit(solution)/shard_map/all_to_all | solution.py:152
  304.2 9.9 %all-to-all-done.3 = bf16[32,1,4,896]{3,2,1,0:T(4,128)(2,1)S(1)} async-done(((bf16[32,1,4,896]{3,2,1,0:T(4,128)(2,1)}), bf16[32,1,4,896]{3,2,1,0:T(4,128)(2,1)S(1)}, u32[]{:S(2)}, u32[]{:S(2)}) %all-to-all-start.3) | async-done | bytes 229408 | tf_op jit(solution)/shard_map/all_to_all | solution.py:152
  315.3 12.8 %all_gather.10 = bf16[16,7168]{1,0:T(8,128)(2,1)S(1)} all-gather(bf16[16,896]{1,0:T(8,128)(2,1)S(1)} %fusion.193), channel_id=1, replica_groups=mesh['dp'=32,'ep'=8] {'ep'}, dimensions={1}, use_global_device_ids=true | all-gather | bytes 258048 | tf_op jit(solution)/shard_map/all_gather | solution.py:159
  335.1 49.9 %all_to_all.42 = bf16[32,1,4,7168]{3,2,1,0:T(4,128)(2,1)S(1)} all-to-all(bf16[32,1,4,7168]{3,2,1,0:T(4,128)(2,1)} %bitcast.418), channel_id=1, replica_groups=mesh['dp'=32,'ep'=8] {'dp'}, dimensions={0} | all-to-all | bytes 3670016 | tf_op jit(solution)/shard_map/all_to_all | solution.py:140
  387.2 4.9 fusion.2
  392.1 9.7 %copy.321 = bf16[32,1,4,7168]{0,2,1,3:T(4,128)(2,1)} copy(bf16[32,1,4,7168]{3,0,2,1:T(8,128)(2,1)} %fusion.2) | data formatting | bytes 3670016
  401.8 9.5 %reshape.617 = bf16[7168,128]{1,0:T(8,128)(2,1)} reshape(bf16[7168,1,4,32]{3,2,1,0:T(4,128)(2,1)} %bitcast.413) | data formatting | bytes 3670016
  432.5 10.9 %reduce-scatter.17.cloned.1.call-done = bf16[896,128]{1,0:T(8,128)(2,1)} async-done(((bf16[7168,128]{1,0:T(8,128)(2,1)}), bf16[896,128]{1,0:T(8,128)(2,1)}) %reduce-scatter.17.cloned.1.call-update) | async-done | bytes 229392
  448.5 10.0 %all-to-all-start.5 = ((bf16[32,1,4,896]{3,2,1,0:T(4,128)(2,1)}), bf16[32,1,4,896]{3,2,1,0:T(4,128)(2,1)S(1)}, u32[]{:S(2)}, u32[]{:S(2)}) async-start(bf16[32,1,4,896]{3,2,1,0:T(4,128)(2,1)} %copy.294), calls=%async_computation.5 | async-start | bytes 458752 | tf_op jit(solution)/shard_map/all_to_all | solution.py:152
  461.0 8.0 %all-to-all-done.5 = bf16[32,1,4,896]{3,2,1,0:T(4,128)(2,1)S(1)} async-done(((bf16[32,1,4,896]{3,2,1,0:T(4,128)(2,1)}), bf16[32,1,4,896]{3,2,1,0:T(4,128)(2,1)S(1)}, u32[]{:S(2)}, u32[]{:S(2)}) %all-to-all-start.5) | async-done | bytes 229408 | tf_op jit(solution)/shard_map/all_to_all | solution.py:152
  470.9 12.8 %all_gather.11 = bf16[16,7168]{1,0:T(8,128)(2,1)S(1)} all-gather(bf16[16,896]{1,0:T(8,128)(2,1)S(1)} %fusion.194), channel_id=1, replica_groups=mesh['dp'=32,'ep'=8] {'ep'}, dimensions={1}, use_global_device_ids=true | all-gather | bytes 258048 | tf_op jit(solution)/shard_map/all_gather | solution.py:159
  492.2 5.2 all-to-all-start.6
  508.9 55.1 %all-reduce.7.cloned.1.call-done = (bf16[16,576]{1,0:T(8,128)(2,1)}, bf16[16,576]{1,0:T(8,128)(2,1)}, bf16[16,576]{1,0:T(8,128)(2,1)}, bf16[16,576]{1,0:T(8,128)(2,1)}) async-done(((bf16[16,576]{1,0:T(8,128)(2,1)}, bf16[16,576]{1,0:T(8,128)(2,1)}, bf16[16,576]{1,0:T(8,128)(2,1)}, bf16[16,576]{1,0:T(8,128)(2,1)}), (bf16[16,576]{1,0:T(8,128)(2,1)}, bf16[16,576]{1,0:T(8,128)(2,1)}, bf16[16,576]{1,0:T(8,128)(2,1)}, ...) | async-done | bytes 73744
  570.6 4.9 fusion.3
  575.6 9.7 %copy.323 = bf16[32,1,4,7168]{0,2,1,3:T(4,128)(2,1)} copy(bf16[32,1,4,7168]{3,0,2,1:T(8,128)(2,1)} %fusion.3) | data formatting | bytes 3670016
  585.2 9.5 %reshape.619 = bf16[7168,128]{1,0:T(8,128)(2,1)} reshape(bf16[7168,1,4,32]{3,2,1,0:T(4,128)(2,1)} %bitcast.414) | data formatting | bytes 3670016
  607.3 23.9 %reduce-scatter.19.cloned.1.call-done = bf16[896,128]{1,0:T(8,128)(2,1)} async-done(((bf16[7168,128]{1,0:T(8,128)(2,1)}), bf16[896,128]{1,0:T(8,128)(2,1)}) %reduce-scatter.19.cloned.1.call-update) | async-done | bytes 229392
  634.8 10.0 %all-to-all-start.7 = ((bf16[32,1,4,896]{3,2,1,0:T(4,128)(2,1)}), bf16[32,1,4,896]{3,2,1,0:T(4,128)(2,1)S(1)}, u32[]{:S(2)}, u32[]{:S(2)}) async-start(bf16[32,1,4,896]{3,2,1,0:T(4,128)(2,1)} %copy.301), calls=%async_computation.7 | async-start | bytes 458752 | tf_op jit(solution)/shard_map/all_to_all | solution.py:152
  648.3 7.0 %all-to-all-done.7 = bf16[32,1,4,896]{3,2,1,0:T(4,128)(2,1)S(1)} async-done(((bf16[32,1,4,896]{3,2,1,0:T(4,128)(2,1)}), bf16[32,1,4,896]{3,2,1,0:T(4,128)(2,1)S(1)}, u32[]{:S(2)}, u32[]{:S(2)}) %all-to-all-start.7) | async-done | bytes 229408 | tf_op jit(solution)/shard_map/all_to_all | solution.py:152
  (264 shorter events, 124.7 us)
Async XLA Ops:
  7.2 73.3 %copy-start = (bf16[1,128,7168]{2,1,0:T(8,128)(2,1)S(1)}, bf16[1,128,7168]{2,1,0:T(8,128)(2,1)}, u32[]{:S(2)}) copy-start(bf16[1,128,7168]{2,1,0:T(8,128)(2,1)} %param.25) | copy-start | bytes 5505028
  7.2 130.2 %reduce-scatter.13.cloned.1.call-start = ((), (), s32[]{:S(2)}) async-start(), calls=%async_computation.12 | async-start | bytes 2064384
  8.0 296.1 %copy-start.33 = (pred[16]{0:T(512)(128)(4,1)}, pred[16]{0:T(512)(128)(4,1)S(1)}, u32[]{:S(2)}) copy-start(pred[16]{0:T(512)(128)(4,1)S(1)} %iota_compare_fusion.13) | copy-start | bytes 52
  12.9 9.1 %copy-start.32 = (s32[16,8]{1,0:T(8,128)}, s32[16,8]{1,0:T(8,128)S(1)}, u32[]{:S(2)}) copy-start(s32[16,8]{1,0:T(8,128)S(1)} %copy.290) | copy-start | bytes 1540
  13.0 9.0 %copy-start.31 = (s32[16,8]{1,0:T(8,128)}, s32[16,8]{1,0:T(8,128)S(1)}, u32[]{:S(2)}) copy-start(s32[16,8]{1,0:T(8,128)S(1)} %copy.297) | copy-start | bytes 1540
  15.2 91.2 %copy-start.8 = (bf16[16,7168]{1,0:T(8,128)(2,1)}, bf16[16,7168]{1,0:T(8,128)(2,1)S(1)}, u32[]{:S(2)}) copy-start(bf16[16,7168]{1,0:T(8,128)(2,1)S(1)} %multiply_convert_fusion.3) | copy-start | bytes 688132
  22.0 57.6 %copy-start.42 = (bf16[1,7168,128]{2,1,0:T(8,128)(2,1)S(1)}, bf16[1,7168,128]{2,1,0:T(8,128)(2,1)}, u32[]{:S(2)}) copy-start(bf16[1,7168,128]{2,1,0:T(8,128)(2,1)} %param.23) | copy-start | bytes 5505028
  106.7 69.0 %copy-start.19 = (f32[7168]{0:T(1024)S(1)}, f32[7168]{0:T(1024)}, u32[]{:S(2)}) copy-start(f32[7168]{0:T(1024)} %param.19) | copy-start | bytes 86020
  141.0 20.6 %all-to-all-start.1 = ((bf16[32,1,4,896]{3,2,1,0:T(4,128)(2,1)}), bf16[32,1,4,896]{3,2,1,0:T(4,128)(2,1)S(1)}, u32[]{:S(2)}, u32[]{:S(2)}) async-start(bf16[32,1,4,896]{3,2,1,0:T(4,128)(2,1)} %copy.280), calls=%async_computation.1 | async-start | bytes 458752 | tf_op jit(solution)/shard_map/all_to_all | solution.py:152
  151.1 138.9 %reduce-scatter.15.cloned.1.call-start = ((), (), s32[]{:S(2)}) async-start(), calls=%async_computation.13 | async-start | bytes 2064384
  162.7 19.2 %copy-start.20 = (bf16[16,896]{1,0:T(8,128)(2,1)}, bf16[16,896]{1,0:T(8,128)(2,1)S(1)}, u32[]{:S(2)}) copy-start(bf16[16,896]{1,0:T(8,128)(2,1)S(1)} %fusion.192) | copy-start | bytes 86020
  175.8 83.1 %copy-start.9 = (bf16[16,7168]{1,0:T(8,128)(2,1)}, bf16[16,7168]{1,0:T(8,128)(2,1)S(1)}, u32[]{:S(2)}) copy-start(bf16[16,7168]{1,0:T(8,128)(2,1)S(1)} %multiply_convert_fusion.2) | copy-start | bytes 688132
  181.8 51.2 %copy-start.43 = (bf16[1,7168,128]{2,1,0:T(8,128)(2,1)S(1)}, bf16[1,7168,128]{2,1,0:T(8,128)(2,1)}, u32[]{:S(2)}) copy-start(bf16[1,7168,128]{2,1,0:T(8,128)(2,1)} %param.23) | copy-start | bytes 5505028
  293.6 20.6 %all-to-all-start.3 = ((bf16[32,1,4,896]{3,2,1,0:T(4,128)(2,1)}), bf16[32,1,4,896]{3,2,1,0:T(4,128)(2,1)S(1)}, u32[]{:S(2)}, u32[]{:S(2)}) async-start(bf16[32,1,4,896]{3,2,1,0:T(4,128)(2,1)} %copy.287), calls=%async_computation.3 | async-start | bytes 458752 | tf_op jit(solution)/shard_map/all_to_all | solution.py:152
  303.6 139.7 %reduce-scatter.17.cloned.1.call-start = ((), (), s32[]{:S(2)}) async-start(), calls=%async_computation.14 | async-start | bytes 2064384
  315.3 19.9 %copy-start.21 = (bf16[16,896]{1,0:T(8,128)(2,1)}, bf16[16,896]{1,0:T(8,128)(2,1)S(1)}, u32[]{:S(2)}) copy-start(bf16[16,896]{1,0:T(8,128)(2,1)S(1)} %fusion.193) | copy-start | bytes 86020
  335.1 51.2 %copy-start.44 = (bf16[1,7168,128]{2,1,0:T(8,128)(2,1)S(1)}, bf16[1,7168,128]{2,1,0:T(8,128)(2,1)}, u32[]{:S(2)}) copy-start(bf16[1,7168,128]{2,1,0:T(8,128)(2,1)} %param.23) | copy-start | bytes 5505028
  411.4 7.9 %copy-start.3 = (bf16[896,576]{0,1:T(8,128)(2,1)S(1)}, bf16[896,576]{0,1:T(8,128)(2,1)}, u32[]{:S(2)}) copy-start(bf16[896,576]{0,1:T(8,128)(2,1)} %param.20) | copy-start | bytes 3096580
  419.3 9.6 %copy-start.23 = (pred[2,1024]{1,0:T(4,128)(4,1)}, pred[2,1024]{1,0:T(4,128)(4,1)S(1)}, u32[]{:S(2)}) copy-start(pred[2,1024]{1,0:T(4,128)(4,1)S(1)} %iota_compare_fusion.12) | copy-start | bytes 6148
  419.3 5.6 copy-start.1
  419.3 5.6 copy-start.18
  448.5 20.5 %all-to-all-start.5 = ((bf16[32,1,4,896]{3,2,1,0:T(4,128)(2,1)}), bf16[32,1,4,896]{3,2,1,0:T(4,128)(2,1)S(1)}, u32[]{:S(2)}, u32[]{:S(2)}) async-start(bf16[32,1,4,896]{3,2,1,0:T(4,128)(2,1)} %copy.294), calls=%async_computation.5 | async-start | bytes 458752 | tf_op jit(solution)/shard_map/all_to_all | solution.py:152
  470.9 13.0 %copy-start.22 = (bf16[16,896]{1,0:T(8,128)(2,1)}, bf16[16,896]{1,0:T(8,128)(2,1)S(1)}, u32[]{:S(2)}) copy-start(bf16[16,896]{1,0:T(8,128)(2,1)S(1)} %fusion.194) | copy-start | bytes 86020
  492.2 75.5 %all-to-all-start.6 = ((bf16[32,1,4,7168]{3,2,1,0:T(4,128)(2,1)}), bf16[32,1,4,7168]{3,2,1,0:T(4,128)(2,1)}, u32[]{:S(2)}, u32[]{:S(2)}) async-start(bf16[32,1,4,7168]{3,2,1,0:T(4,128)(2,1)} %bitcast.415), calls=%async_computation.6 | async-start | bytes 3670016 | tf_op jit(solution)/shard_map/all_to_all | solution.py:140
  497.4 66.7 %all-reduce.7.cloned.1.call-start = ((), (), s32[]{:S(2)}) async-start(), calls=%async_computation.16 | async-start | bytes 163840
  502.7 128.6 %reduce-scatter.19.cloned.1.call-start = ((), (), s32[]{:S(2)}) async-start(), calls=%async_computation.15 | async-start | bytes 2064384
  634.8 20.5 %all-to-all-start.7 = ((bf16[32,1,4,896]{3,2,1,0:T(4,128)(2,1)}), bf16[32,1,4,896]{3,2,1,0:T(4,128)(2,1)S(1)}, u32[]{:S(2)}, u32[]{:S(2)}) async-start(bf16[32,1,4,896]{3,2,1,0:T(4,128)(2,1)} %copy.301), calls=%async_computation.7 | async-start | bytes 458752 | tf_op jit(solution)/shard_map/all_to_all | solution.py:152
  644.9 10.5 %copy-start.34 = (pred[16]{0:T(512)(128)(4,1)S(1)}, pred[16]{0:T(512)(128)(4,1)}, u32[]{:S(2)}) copy-start(pred[16]{0:T(512)(128)(4,1)} %copy-done.33) | copy-start | bytes 52
  644.9 10.5 %copy-start.35 = (f32[16,128]{1,0:T(8,128)S(1)}, f32[16,128]{1,0:T(8,128)}, u32[]{:S(2)}) copy-start(f32[16,128]{1,0:T(8,128)} %select_reduce_fusion.8) | copy-start | bytes 24580
  647.4 9.1 %copy-start.28 = (bf16[1,16,896]{2,1,0:T(8,128)(2,1)S(1)}, bf16[1,16,896]{2,1,0:T(8,128)(2,1)}, u32[]{:S(2)}) copy-start(bf16[1,16,896]{2,1,0:T(8,128)(2,1)} %get-tuple-element.61) | copy-start | bytes 86020
  647.4 9.1 %copy-start.29 = (bf16[1,16,896]{2,1,0:T(8,128)(2,1)S(1)}, bf16[1,16,896]{2,1,0:T(8,128)(2,1)}, u32[]{:S(2)}) copy-start(bf16[1,16,896]{2,1,0:T(8,128)(2,1)} %get-tuple-element.62) | copy-start | bytes 86020
  647.4 9.1 %copy-start.30 = (bf16[1,16,896]{2,1,0:T(8,128)(2,1)S(1)}, bf16[1,16,896]{2,1,0:T(8,128)(2,1)}, u32[]{:S(2)}) copy-start(bf16[1,16,896]{2,1,0:T(8,128)(2,1)} %get-tuple-element.63) | copy-start | bytes 86020
  (24 other events, 68.0 us)
Sparse Core Ops, SparseCore 0:
  104.8 32.5 reduce-scatter.12
  258.2 31.7 reduce-scatter.14
  411.5 31.8 reduce-scatter.16
  502.8 61.2 all-reduce.6
  595.0 36.2 reduce-scatter.18
where the time goes:
time: 676 us; the launch traced here: 664 us
  blocking collectives  195 us (29%)
  waiting for transfers between devices  186 us (28%)
  local copies, waits for them, and re-layouts  124 us (18%)
  matrix products  69.1 us (10%)
  starting transfers between devices  45.8 us (7%)
  other arithmetic  27.5 us (4%)
  between operations  16.5 us (2%)
    all_to_all x3, blocking collectives, shards(): lax.all_to_all(outgoing, 'dp', split_axis=0, concat_axis=0, tiled=True)  156 us
    unnamed x10, waiting for transfers between devices  151 us
    unnamed x105, local copies, waits for them, and re-layouts  93.5 us
    all_to_all x4, starting transfers between devices, shards(): lax.all_to_all(summed, 'dp', split_axis=0, concat_axis=0, tiled=True)  40.1 us
    all_gather x3, blocking collectives, shards(): hidden_state = lax.all_gather(new_slice, 'ep', axis=1, tiled=True)  38.5 us
    all_to_all x4, waiting for transfers between devices, shards(): lax.all_to_all(summed, 'dp', split_axis=0, concat_axis=0, tiled=True)  34.9 us
    dot_general x4, matrix products, shards(): jnp.einsum('sekf,efd->sekd', hidden_units, w_down, preferred_element_type...  19.7 us
    reshape x4, local copies, waits for them, and re-layouts, shards(): outgoing.reshape(rank_count, local_experts, capacity, model_width)  16.2 us
  transfers between devices with their start and end apart: 10, of which 9 were waited for; matrix products, arithmetic and copies ran while one was open for 8% of the time, Pallas kernels for 0%

commit v1 on v0

v1 whole, which is shorter than its diff:
```python
import functools

import jax
import jax.numpy as jnp
from jax import lax
from jax.experimental import pallas as pl
from jax.experimental.pallas import tpu as pltpu
from jax.sharding import PartitionSpec as P

LAT = 512
KD = 576
TOP = 8
STEPS = 4
CAP = 4
SLOTS = 16
LANES = 128
BLOCKS = 7
SHARE = BLOCKS * LANES
MEMBERS = 8
RING = 4
EXPERTS = 32
WIDTH = SHARE * MEMBERS
UNITS = 128
HEADS = 64
CTX = 1024
REQ = 2
GROUPS = 4
ROWS = 32
HALF = ROWS // 2
OFFSETS = (0, 1, 7, 2, 6, 3, 5, 4)

SCALE = 0.07216878364870322
ROUTE_SCALE = 2.827
EPSILON = 1e-06
THETA = 50000.0
NEGATIVE = -1e30
LIFT = 2.0**60

BF16 = jnp.bfloat16
F32 = jnp.float32
MESH = pl.DeviceIdType.MESH


def iota(shape, axis):
    return lax.broadcasted_iota(jnp.int32, shape, axis)


def kernel(
    counts_ref,
    lengths_ref,
    routes_ref,
    gain_ref,
    rgain_ref,
    kv_gain_ref,
    rope_ref,
    drafts_hbm,
    cache_hbm,
    queries_hbm,
    kv_hbm,
    gate_hbm,
    up_hbm,
    down_hbm,
    drafted_ref,
    attended_ref,
    cache,
    queries,
    kv,
    wgu,
    wd,
    start,
    x_ref,
    table,
    table_t,
    perm,
    tri,
    a_out,
    a_in,
    rows_in,
    share,
    sib_in,
    opp_out,
    opp_in,
    near_out,
    near_in,
    gates,
    d_out,
    d_in,
    lat_out,
    lat_in,
    keys,
    part_o,
    part_m,
    part_l,
    load_sem,
    a_send,
    a_recv,
    b_send,
    b_near,
    b_opp,
    b_sib,
    c_send,
    c_sib,
    c_opp,
    c_near,
    d_send,
    d_recv,
    l_send,
    l_recv,
):
    dp = lax.axis_index("dp")
    ep = lax.axis_index("ep")
    z, xx = dp // RING, dp % RING
    y, core = ep // 2, ep % 2
    y_up, y_down, y_far = (y + 1) % RING, (y + RING - 1) % RING, (y + 2) % RING
    other = 1 - core
    sibling = 2 * y + other
    ep_up, ep_down = 2 * y_up + core, 2 * y_down + core
    count = counts_ref[0]

    def rank_at(i, dx, sign):
        zt = (z + 8 + sign * OFFSETS[i]) % 8
        xt = (xx + 4 + sign * dx) % 4
        return zt * RING + xt

    def load(src, dst, n):
        return pltpu.make_async_copy(src, dst, load_sem.at[n])

    loads = [
        load(
            drafts_hbm.at[:, pl.ds(pl.multiple_of(ep * SHARE, SHARE), SHARE)], start, 0
        ),
        load(kv_hbm, kv, 1),
        load(gate_hbm.at[0], wgu.at[:, 0:UNITS], 2),
        load(up_hbm.at[0], wgu.at[:, UNITS : 2 * UNITS], 3),
        load(down_hbm.at[0], wd, 4),
        load(cache_hbm, cache, 5),
        load(queries_hbm, queries, 6),
    ]
    for item in loads:
        item.start()

    barrier = pltpu.get_barrier_semaphore()
    for n in range(1, EXPERTS):
        pl.semaphore_signal(
            barrier, inc=1, device_id=((dp + n) % EXPERTS, ep), device_id_type=MESH
        )
    for n in range(1, MEMBERS):
        pl.semaphore_signal(
            barrier, inc=1, device_id=(dp, (ep + n) % MEMBERS), device_id_type=MESH
        )

    r = iota((256, 256), 0)
    c = iota((256, 256), 1)
    perm[...] = jnp.where(
        c == ((r >> 2) & 7) * 32 + (r >> 5) * 4 + (r & 3), 1.0, 0.0
    ).astype(BF16)
    r = iota((LANES, LANES), 0)
    c = iota((LANES, LANES), 1)
    tri[...] = jnp.where(((r >> 4) == (c >> 4)) & ((r & 15) < (c & 15)), 1.0, 0.0).astype(BF16)
    pr = iota((32, LANES), 0)
    pc = iota((32, LANES), 1)
    pattern = jnp.where((pr >> 2) == (pc >> 4), pr & 3, -7).astype(F32)

    def build_table(s):
        expert = iota((EXPERTS, LANES), 0)
        live = (iota((EXPERTS, LANES), 1) & 15) < count
        named = routes_ref[s]
        hit = expert == named[0:1, :]
        for k in range(1, TOP):
            hit = hit | (expert == named[k : k + 1, :])
        hit = hit & live
        before = jnp.dot(
            jnp.where(hit, 1.0, 0.0).astype(BF16), tri[...], preferred_element_type=F32
        )
        place = jnp.where(hit, before, -1.0)
        for e in range(EXPERTS):
            table[e * 32 : e * 32 + 32, :] = jnp.where(
                jnp.broadcast_to(place[e : e + 1, :], (32, LANES)) == pattern, 1.0, 0.0
            ).astype(BF16)

    def transpose_table():
        for n in range(8):
            table_t[:, n * LANES : (n + 1) * LANES] = (
                table[n * LANES : (n + 1) * LANES, :].astype(F32).T.astype(BF16)
            )

    build_table(0)
    lat_out[...] = jnp.zeros_like(lat_out)
    keys[...] = jnp.zeros_like(keys)
    loads[0].wait()
    for j in range(BLOCKS):
        x_ref[j * SLOTS : (j + 1) * SLOTS, :] = start[:, j * LANES : (j + 1) * LANES].astype(F32)
    x_ref[BLOCKS * SLOTS :, :] = jnp.zeros((SLOTS, LANES), F32)
    pl.semaphore_wait(barrier, EXPERTS - 1 + MEMBERS - 1)

    def remote(src, dst, send, recv, device):
        pltpu.make_async_remote_copy(
            src_ref=src,
            dst_ref=dst,
            send_sem=send,
            recv_sem=recv,
            device_id=device,
            device_id_type=MESH,
        ).start()

    def arrive(ref, sem):
        pltpu.make_async_copy(ref, ref, sem).wait()

    def step(s, carry):
        parity = s % 2
        xb = x_ref[...].astype(BF16)
        for i in range(8):
            zt = (z + OFFSETS[i]) % 8
            rows = table[pl.ds(pl.multiple_of(zt * LANES, LANES), LANES), :]
            picked = jnp.dot(rows, xb, preferred_element_type=F32).astype(BF16)
            a_out[pl.ds(zt * RING, RING)] = picked.reshape(RING, 32, LANES)
            for dx in range(4):
                p = i * 4 + dx
                target = rank_at(i, dx, 1)
                if p == 0:
                    pltpu.make_async_copy(
                        a_out.at[target], a_in.at[0], a_recv.at[0]
                    ).start()
                else:
                    remote(
                        a_out.at[target], a_in.at[p], a_send, a_recv.at[p // 8], (target, ep)
                    )

        def latent_send():
            @pl.when(s == 0)
            def _():
                loads[1].wait()

            xs = jnp.concatenate(
                [x_ref[j * SLOTS : (j + 1) * SLOTS, :] for j in range(BLOCKS)], axis=1
            )
            gained = (xs * gain_ref[pl.ds(ep, 1), :]).astype(BF16)
            latent = jnp.dot(gained, kv[...], preferred_element_type=F32)
            squares = jnp.broadcast_to(
                jnp.sum(xs * xs, axis=1, keepdims=True), (SLOTS, LANES)
            )
            for t in range(SLOTS):
                row = (t % 2) * 8
                for jb in range(4):
                    lat_out[t // 2, row + jb : row + jb + 1, :] = latent[
                        t : t + 1, jb * LANES : (jb + 1) * LANES
                    ]
                lat_out[t // 2, row + 4 : row + 5, 0:64] = latent[t : t + 1, LAT:KD]
                lat_out[t // 2, row + 5 : row + 6, :] = squares[t : t + 1, :]
            for n in range(1, MEMBERS):
                target = (ep + n) % MEMBERS
                remote(
                    lat_out.at[target],
                    lat_in.at[parity, ep],
                    l_send,
                    l_recv.at[parity],
                    (dp, target),
                )
            lat_in[parity, ep] = lat_out[ep]

        def latent_take():
            arrive(lat_in.at[parity, pl.ds(0, MEMBERS - 1)], l_recv.at[parity])
            total = lat_in[parity, 0]
            for n in range(1, MEMBERS):
                total = total + lat_in[parity, n]
            scale = lax.rsqrt(total[5:6, :] * (1.0 / WIDTH) + EPSILON)
            scale_second = lax.rsqrt(total[13:14, :] * (1.0 / WIDTH) + EPSILON)
            which = iota((16, LANES), 0) < 8
            raw = total * jnp.where(
                which,
                jnp.broadcast_to(scale, (16, LANES)),
                jnp.broadcast_to(scale_second, (16, LANES)),
            )
            rope = rope_ref[s]
            ahead = pltpu.roll(raw, LANES - 32, 1)
            behind = pltpu.roll(raw, 32, 1)
            for q in range(REQ):
                base = q * 8
                lat = raw[base : base + 4, :]
                mean = jnp.sum(
                    jnp.sum(lat * lat, axis=1, keepdims=True), axis=0, keepdims=True
                ) * (1.0 / LAT)
                lat = lat * lax.rsqrt(mean + EPSILON) * kv_gain_ref[...]
                for jb in range(4):
                    keys[q, jb, pl.ds(s, 1), :] = lat[jb : jb + 1, :]
                keys[q, 4, pl.ds(s, 1), :] = (
                    raw[base + 4 : base + 5, :] * rope[q : q + 1, :]
                    + ahead[base + 4 : base + 5, :] * rope[2 + q : 3 + q, :]
                    + behind[base + 4 : base + 5, :] * rope[4 + q : 5 + q, :]
                )

        def attend_cache(q):
            query = queries[s, q]
            held = cache[q]
            score = SCALE * lax.dot_general(
                query, held, (((1,), (1,)), ((), ())), preferred_element_type=F32
            )
            valid = iota((HEADS, CTX), 1) < lengths_ref[q]
            score = jnp.where(valid, score, NEGATIVE)
            top = jnp.max(score, axis=1, keepdims=True)
            prob = jnp.where(valid, jnp.exp(score - top), 0.0)
            part_m[q] = jnp.broadcast_to(top, (HEADS, LANES))
            part_l[q] = jnp.broadcast_to(jnp.sum(prob, axis=1, keepdims=True), (HEADS, LANES))
            part_o[q] = jnp.dot(prob.astype(BF16), held[:, :LAT], preferred_element_type=F32)

        def attend_draft(q):
            query = queries[s, q]
            fresh = jnp.concatenate([keys[q, jb] for jb in range(5)], axis=1).astype(BF16)
            score = SCALE * lax.dot_general(
                query, fresh[:, :KD], (((1,), (1,)), ((), ())), preferred_element_type=F32
            )
            valid = iota((HEADS, 8), 1) <= s
            score = jnp.where(valid, score, NEGATIVE)
            old_top = part_m[q][:, 0:1]
            top = jnp.maximum(jnp.max(score, axis=1, keepdims=True), old_top)
            prob = jnp.where(valid, jnp.exp(score - top), 0.0)
            shrink = jnp.exp(old_top - top)
            total = part_l[q][:, 0:1] * shrink + jnp.sum(prob, axis=1, keepdims=True)
            out = part_o[q] * shrink + jnp.dot(
                prob.astype(BF16), fresh[:, :LAT], preferred_element_type=F32
            )
            out = out / total
            own = (ep * REQ + q) < count
            attended_ref[s, q] = jnp.where(own, out, 0.0).astype(BF16)

        def gather_start(g):
            arrive(a_in.at[pl.ds(g * 8, 8)], a_recv.at[g])
            block = a_in[pl.ds(g * 8, 8)].reshape(256, LANES)
            natural = jnp.dot(perm[...], block, preferred_element_type=F32).astype(BF16)
            rows = pl.ds(g * ROWS, ROWS)
            for j in range(BLOCKS):
                rows_in[ep, rows, j * LANES : (j + 1) * LANES] = natural[
                    j * ROWS : (j + 1) * ROWS, :
                ]
            mine = rows_in.at[ep, rows]
            remote(mine, mine, b_send.at[g], b_near.at[g, 0], (dp, ep_up))
            remote(mine, mine, b_send.at[g], b_near.at[g, 1], (dp, ep_down))
            remote(mine, mine, b_send.at[g], b_sib.at[g, 0], (dp, sibling))

        def gather_pass(g):
            rows = pl.ds(g * ROWS, ROWS)
            first = pl.ds(g * ROWS, HALF)
            second = pl.ds(g * ROWS + HALF, HALF)
            got = rows_in.at[ep_down, rows]
            arrive(got, b_near.at[g, 0])
            part = rows_in.at[ep_down, first]
            remote(part, part, b_send.at[g], b_opp.at[g, 0], (dp, ep_up))
            remote(got, got, b_send.at[g], b_sib.at[g, 1], (dp, sibling))
            got = rows_in.at[ep_up, rows]
            arrive(got, b_near.at[g, 1])
            part = rows_in.at[ep_up, second]
            remote(part, part, b_send.at[g], b_opp.at[g, 1], (dp, ep_down))
            remote(got, got, b_send.at[g], b_sib.at[g, 2], (dp, sibling))

        def gather_end(g):
            far = 2 * y_far + core
            arrive(rows_in.at[far, pl.ds(g * ROWS, HALF)], b_opp.at[g, 0])
            arrive(rows_in.at[far, pl.ds(g * ROWS + HALF, HALF)], b_opp.at[g, 1])
            got = rows_in.at[far, pl.ds(g * ROWS, ROWS)]
            remote(got, got, b_send.at[g], b_sib.at[g, 3], (dp, sibling))

        def expert(g):
            rows = slice(g * ROWS, (g + 1) * ROWS)
            if g == 0:

                @pl.when(s == 0)
                def _():
                    loads[2].wait()
                    loads[3].wait()
                    loads[4].wait()

            for n in range(4):
                arrive(rows_in.at[0, pl.ds(g * ROWS, ROWS)], b_sib.at[g, n])
            total = jnp.zeros((ROWS, 2 * UNITS), F32)
            squares = jnp.zeros((ROWS, LANES), F32)
            logits = jnp.zeros((ROWS, LANES), F32)
            for e in range(MEMBERS):
                wide = rows_in[e, rows, :].astype(F32)
                gained = (wide * gain_ref[e : e + 1, :]).astype(BF16)
                total = total + jnp.dot(
                    gained, wgu[e * SHARE : (e + 1) * SHARE, :], preferred_element_type=F32
                )
                sq = wide * wide
                lg = wide * rgain_ref[e : e + 1, :]
                for j in range(BLOCKS):
                    squares = squares + sq[:, j * LANES : (j + 1) * LANES]
                    logits = logits + lg[:, j * LANES : (j + 1) * LANES]
            scale = lax.rsqrt(
                jnp.sum(squares, axis=1, keepdims=True) * (1.0 / WIDTH) + EPSILON
            )
            logit = jnp.sum(logits, axis=1, keepdims=True) * scale
            gates[g] = jnp.broadcast_to(LIFT / (1.0 + jnp.exp(-logit)), (ROWS, LANES))
            total = total * scale
            first = total[:, :UNITS]
            hidden = (first / (1.0 + jnp.exp(-first)) * total[:, UNITS:]).astype(BF16)
            for e in range(MEMBERS):
                share[g, e % 2, e // 2] = jnp.dot(
                    hidden, wd[:, e * SHARE : (e + 1) * SHARE], preferred_element_type=F32
                ).astype(BF16)
            remote(share.at[g, other], sib_in.at[g], c_send.at[g], c_sib.at[g], (dp, sibling))

        def pair(g, to):
            return share[g, core, to].astype(F32) + sib_in[g, to].astype(F32)

        def scatter_far(g):
            arrive(rows_in.at[pl.ds(0, 7), pl.ds(0, ROWS)], b_send.at[g])
            arrive(sib_in.at[g], c_sib.at[g])
            opp_out[g] = pair(g, y_far).astype(BF16)
            remote(
                opp_out.at[g, pl.ds(0, HALF)],
                opp_in.at[g, 0],
                c_send.at[g],
                c_opp.at[g, 0],
                (dp, ep_up),
            )
            remote(
                opp_out.at[g, pl.ds(HALF, HALF)],
                opp_in.at[g, 1],
                c_send.at[g],
                c_opp.at[g, 1],
                (dp, ep_down),
            )

        def scatter_near(g):
            total = pair(g, y_up)
            arrive(opp_in.at[g, 0], c_opp.at[g, 0])
            near_out[g, 0, 0:HALF, :] = (total[:HALF] + opp_in[g, 0].astype(F32)).astype(BF16)
            near_out[g, 0, HALF:ROWS, :] = total[HALF:].astype(BF16)
            remote(near_out.at[g, 0], near_in.at[g, 0], c_send.at[g], c_near.at[g, 0], (dp, ep_up))
            total = pair(g, y_down)
            arrive(opp_in.at[g, 1], c_opp.at[g, 1])
            near_out[g, 1, 0:HALF, :] = total[:HALF].astype(BF16)
            near_out[g, 1, HALF:ROWS, :] = (total[HALF:] + opp_in[g, 1].astype(F32)).astype(BF16)
            remote(
                near_out.at[g, 1], near_in.at[g, 1], c_send.at[g], c_near.at[g, 1], (dp, ep_down)
            )

        def give_back(g):
            total = pair(g, y)
            arrive(near_in.at[g, 0], c_near.at[g, 0])
            arrive(near_in.at[g, 1], c_near.at[g, 1])
            total = total + near_in[g, 0].astype(F32) + near_in[g, 1].astype(F32)
            gate = gates[g]
            parts = [
                (total[:, j * LANES : (j + 1) * LANES] * gate).astype(BF16)
                for j in range(BLOCKS)
            ]
            parts.append(gate.astype(BF16))
            block = jnp.dot(
                perm[...], jnp.concatenate(parts, axis=0), preferred_element_type=F32
            ).astype(BF16)
            d_out[pl.ds(g * 8, 8)] = block.reshape(8, 32, LANES)
            for n in range(8):
                p = g * 8 + n
                target = rank_at(p // 4, p % 4, -1)
                if p == 0:
                    pltpu.make_async_copy(d_out.at[0], d_in.at[dp], d_recv).start()
                else:
                    remote(d_out.at[p], d_in.at[dp], d_send, d_recv, (target, ep))

        latent_send()
        transpose_table()
        stages = [
            gather_start,
            gather_pass,
            gather_end,
            expert,
            scatter_far,
            scatter_near,
            give_back,
        ]
        for tick in range(GROUPS + len(stages) - 1):
            for k in (1, 2, 0, 6, 5, 4, 3):
                g = tick - k
                if 0 <= g < GROUPS:
                    stages[k](g)

        @pl.when(s == 0)
        def _():
            loads[5].wait()
            loads[6].wait()

        latent_take()
        for q in range(REQ):
            attend_cache(q)
            attend_draft(q)
        build_table(jnp.minimum(s + 1, STEPS - 1))

        arrive(d_in, d_recv)
        summed = jnp.dot(
            table_t[...], d_in[...].reshape(EXPERTS * 32, LANES), preferred_element_type=F32
        )
        weight = summed[BLOCKS * SLOTS :, :]
        alive = weight > 0.0
        factor = jnp.where(alive, ROUTE_SCALE / jnp.where(alive, weight, 1.0), 0.0)
        shown = iota((SLOTS, LANES), 0) < count
        for j in range(BLOCKS):
            rows = slice(j * SLOTS, (j + 1) * SLOTS)
            update = jnp.where(alive, summed[rows, :] * factor, 0.0)
            fresh = (x_ref[rows, :] + update).astype(BF16).astype(F32)
            x_ref[rows, :] = fresh
            drafted_ref[s, :, j * LANES : (j + 1) * LANES] = jnp.where(shown, fresh, 0.0).astype(
                BF16
            )

        arrive(a_out.at[pl.ds(0, EXPERTS - 1)], a_send)
        arrive(d_out.at[pl.ds(0, EXPERTS - 1)], d_send)
        arrive(lat_out.at[pl.ds(0, MEMBERS - 1)], l_send)
        for g in range(GROUPS):
            arrive(rows_in.at[pl.ds(0, 7), pl.ds(0, ROWS)], c_send.at[g])
        return carry

    lax.fori_loop(0, STEPS, step, 0)


def shards(
    drafts_in,
    cache,
    queries,
    lengths,
    counts,
    routes,
    norm_gain,
    kv_weight,
    kv_gain,
    router,
    w_gate,
    w_up,
    w_down,
):
    dp = lax.axis_index("dp")
    routes_t = jnp.tile(jnp.swapaxes(routes, 1, 2), (1, 1, LANES // SLOTS))
    gain = norm_gain.reshape(MEMBERS, SHARE)
    column = lax.dynamic_slice_in_dim(router, dp, 1, 1).astype(F32)
    rgain = column.reshape(MEMBERS, SHARE) * gain
    middle = (KD - LAT) // 2
    frequency = THETA ** (-jnp.arange(middle, dtype=F32) / middle)
    position = lengths[None, :] + jnp.arange(STEPS)[:, None]
    angles = position.astype(F32)[:, :, None] * frequency
    cosine, sine = jnp.cos(angles), jnp.sin(angles)
    none = jnp.zeros_like(sine)
    tail = jnp.zeros((STEPS, REQ, LANES - 2 * middle), F32)
    rope = jnp.concatenate(
        [
            jnp.concatenate([cosine, cosine, tail], axis=-1),
            jnp.concatenate([-sine, none, tail], axis=-1),
            jnp.concatenate([none, sine, tail], axis=-1),
            jnp.zeros((STEPS, REQ, LANES), F32),
        ],
        axis=1,
    )
    vmem = pl.BlockSpec(memory_space=pltpu.VMEM)
    smem = pl.BlockSpec(memory_space=pltpu.SMEM)
    hbm = pl.BlockSpec(memory_space=pl.ANY)
    dma = pltpu.SemaphoreType.DMA
    return pl.pallas_call(
        kernel,
        out_shape=(
            jax.ShapeDtypeStruct((STEPS, SLOTS, SHARE), BF16),
            jax.ShapeDtypeStruct((STEPS, REQ, HEADS, LAT), BF16),
        ),
        in_specs=[smem] * 2 + [vmem] * 5 + [hbm] * 7,
        out_specs=(vmem, vmem),
        scratch_shapes=[
            pltpu.VMEM((REQ, CTX, KD), BF16),
            pltpu.VMEM((STEPS, REQ, HEADS, KD), BF16),
            pltpu.VMEM((SHARE, KD), BF16),
            pltpu.VMEM((WIDTH, 2 * UNITS), BF16),
            pltpu.VMEM((UNITS, WIDTH), BF16),
            pltpu.VMEM((SLOTS, SHARE), BF16),
            pltpu.VMEM((LANES, LANES), F32),
            pltpu.VMEM((EXPERTS * 32, LANES), BF16),
            pltpu.VMEM((LANES, EXPERTS * 32), BF16),
            pltpu.VMEM((256, 256), BF16),
            pltpu.VMEM((LANES, LANES), BF16),
            pltpu.VMEM((EXPERTS, 32, LANES), BF16),
            pltpu.VMEM((EXPERTS, 32, LANES), BF16),
            pltpu.VMEM((MEMBERS, LANES, SHARE), BF16),
            pltpu.VMEM((GROUPS, 2, RING, ROWS, SHARE), BF16),
            pltpu.VMEM((GROUPS, RING, ROWS, SHARE), BF16),
            pltpu.VMEM((GROUPS, ROWS, SHARE), BF16),
            pltpu.VMEM((GROUPS, 2, HALF, SHARE), BF16),
            pltpu.VMEM((GROUPS, 2, ROWS, SHARE), BF16),
            pltpu.VMEM((GROUPS, 2, ROWS, SHARE), BF16),
            pltpu.VMEM((GROUPS, ROWS, LANES), F32),
            pltpu.VMEM((EXPERTS, 32, LANES), BF16),
            pltpu.VMEM((EXPERTS, 32, LANES), BF16),
            pltpu.VMEM((MEMBERS, 16, LANES), F32),
            pltpu.VMEM((2, MEMBERS, 16, LANES), F32),
            pltpu.VMEM((REQ, 5, 8, LANES), F32),
            pltpu.VMEM((REQ, HEADS, LAT), F32),
            pltpu.VMEM((REQ, HEADS, LANES), F32),
            pltpu.VMEM((REQ, HEADS, LANES), F32),
            dma((7,)),
            dma,
            dma((GROUPS,)),
            dma((GROUPS,)),
            dma((GROUPS, 2)),
            dma((GROUPS, 2)),
            dma((GROUPS, 4)),
            dma((GROUPS,)),
            dma((GROUPS,)),
            dma((GROUPS, 2)),
            dma((GROUPS, 2)),
            dma,
            dma,
            dma,
            dma((2,)),
        ],
        compiler_params=pltpu.CompilerParams(
            collective_id=0, has_side_effects=True, vmem_limit_bytes=48 * 1024 * 1024
        ),
        name="draft_steps",
    )(
        counts,
        lengths,
        routes_t,
        gain,
        rgain,
        kv_gain.reshape(LAT // LANES, LANES),
        rope,
        drafts_in,
        cache,
        queries,
        kv_weight,
        w_gate,
        w_up,
        w_down,
    )


def solution(mesh):
    return jax.shard_map(
        shards,
        mesh=mesh,
        in_specs=(
            P("dp", None),
            P(("dp", "ep"), None, None),
            P(None, ("dp", "ep"), None, None),
            P(("dp", "ep")),
            P("dp"),
            P(None, "dp", None),
            P(),
            P("ep", None),
            P(),
            P(),
            P("dp", None, "ep"),
            P("dp", None, "ep"),
            P("dp", "ep", None),
        ),
        out_specs=(P(None, "dp", "ep"), P(None, ("dp", "ep"), None, None)),
        check_vma=False,
    )
```

time: 676 us -> 220 us (0.33); the launches traced: 664 us -> 219 us
  Pallas kernels: 0 us -> 205 us
  blocking collectives: 195 us -> 0 us
  waiting for transfers between devices: 186 us -> 0 us
  local copies, waits for them, and re-layouts: 124 us -> 10.7 us
  matrix products: 69.1 us -> 0 us
  starting transfers between devices: 45.8 us -> 0 us
  other arithmetic: 27.5 us -> 1.91 us
  between operations: 16.5 us -> 1.41 us
    pallas_call x0 -> x1, Pallas kernels: none -> 205 us  [shards(): pl.pallas_call(kernel, out_shape=(jax.ShapeDtypeStruct((STEPS, SLOTS, SHA...]
    all_to_all x3 -> x0, blocking collectives: 156 us -> none  [shards(): lax.all_to_all(outgoing, 'dp', split_axis=0, concat_axis=0, tiled=True)]
    unnamed x10 -> x0, waiting for transfers between devices: 151 us -> none
    unnamed x105 -> x14, local copies, waits for them, and re-layouts: 93.5 us -> 9.06 us
    dot_general x39 -> x0, matrix products: 69.1 us -> none  [the longest x4 19.7 us: shards(): jnp.einsum('sekf,efd->sekd', hidden_units, w_down, preferred_element_type...]
    all_to_all x5 -> x0, starting transfers between devices: 45.3 us -> none  [the longest x4 40.1 us: shards(): lax.all_to_all(summed, 'dp', split_axis=0, concat_axis=0, tiled=True)]
    all_gather x3 -> x0, blocking collectives: 38.5 us -> none  [shards(): hidden_state = lax.all_gather(new_slice, 'ep', axis=1, tiled=True)]
    all_to_all x5 -> x0, waiting for transfers between devices: 34.9 us -> none  [the longest x4 34.9 us: shards(): lax.all_to_all(summed, 'dp', split_axis=0, concat_axis=0, tiled=True)]
  transfers between devices with their start and end apart: 10 -> 0, of which waited for: 9 -> 0; matrix products, arithmetic and copies ran while one was open for 8% -> 0% of each run, Pallas kernels for 0% -> 0%
where the time goes in v1:
time: 220 us; the launch traced here: 219 us
  Pallas kernels  205 us (93%)
  local copies, waits for them, and re-layouts  10.7 us (5%)
    pallas_call x1, Pallas kernels, shards(): pl.pallas_call(kernel, out_shape=(jax.ShapeDtypeStruct((STEPS, SLOTS, SHA...  205 us
    unnamed x14, local copies, waits for them, and re-layouts  9.06 us

profile of v1, /device:TPU:32, one launch (start us, length us, event | category | flops | bytes accessed | tf_op | source)
XLA Modules:
  0.0 218.7 jit_solution(594061363914497790)
XLA Ops:
  1.3 0.1 pad.9.clone
  1.4 0.7 add_convert_fusion
  2.0 0.1 multiply_cosine_fusion
  2.2 0.1 maximum_maximum_fusion.rope_ref
  2.3 1.0 convert_reduce_fusion
  3.3 0.8 reshape.45.gain_ref
  4.1 0.7 tile.4
  4.8 0.1 tile.10.routes_ref
  4.9 2.0 copy.16.kv_hbm
  7.0 0.0 copy-start
  7.0 0.0 copy-start.2
  7.0 0.0 copy-start.3
  7.0 0.0 copy-start.4
  7.0 4.5 %copy.15.cache_hbm = bf16[2,1024,576]{2,1,0:T(8,128)(2,1)} copy(bf16[2,1024,576]{1,2,0:T(8,128)(2,1)} %param.14) | data formatting | bytes 4718592 | tf_op args[1]
  11.5 0.0 copy-done
  11.5 0.0 copy-done.2
  11.5 0.0 copy-done.3
  11.5 0.0 copy-done.4
  11.5 0.0 copy-start.1
  11.5 1.1 copy-done.1
  12.6 204.7 %draft_steps.1 = (bf16[4,16,896]{2,1,0:T(8,128)(2,1)S(1)}, bf16[4,2,64,512]{3,2,1,0:T(8,128)(2,1)S(1)}) custom-call(s32[1]{0:T(128)S(6)} %copy.19.counts_ref, s32[2]{0:T(128)S(1)} %copy-done.4, s32[4,8,128]{2,1,0:T(8,128)S(1)} %tile.10.routes_ref, f32[8,896]{1,0:T(8,128)S(1)} %reshape.45.gain_ref, f32[8,896]{1,0:T(8,128)S(1)} %mul.16.rgain_ref, ...), custom_call_target="tpu_custom_call" | custom-call | tf_op jit(solution)/shard_map/draft_steps/pallas_call | solution.py:556
  217.3 0.6 copy.20
  217.9 0.8 copy.21
  (6 shorter events, 0.0 us)
Async XLA Ops:
  7.0 4.5 %copy-start = (bf16[1,7168,128]{2,1,0:T(8,128)(2,1)S(1)}, bf16[1,7168,128]{2,1,0:T(8,128)(2,1)}, u32[]{:S(2)}) copy-start(bf16[1,7168,128]{2,1,0:T(8,128)(2,1)} %gate_hbm.1) | copy-start | bytes 5505028
  7.0 4.5 %copy-start.2 = (bf16[16,7168]{1,0:T(8,128)(2,1)S(1)}, bf16[16,7168]{1,0:T(8,128)(2,1)}, u32[]{:S(2)}) copy-start(bf16[16,7168]{1,0:T(8,128)(2,1)} %drafts_hbm.1) | copy-start | bytes 688132
  7.0 4.5 %copy-start.3 = (f32[512]{0:T(512)S(1)}, f32[512]{0:T(512)}, u32[]{:S(2)}) copy-start(f32[512]{0:T(512)} %param.21) | copy-start | bytes 6148
  7.0 4.5 %copy-start.4 = (s32[2]{0:T(128)S(1)}, s32[2]{0:T(128)}, u32[]{:S(2)}) copy-start(s32[2]{0:T(128)} %lengths_ref.1) | copy-start | bytes 28
  11.5 1.1 copy-start.1

commit v2 on v0

v2 whole, which is shorter than its diff:
```python
import jax
import jax.numpy as jnp
import numpy as np
from jax import lax
from jax.experimental import pallas as pl
from jax.experimental.pallas import tpu as pltpu
from jax.sharding import PartitionSpec as P

LAT = 512
KD = 576
TOP = 8
STEPS = 4
CAP = 4
SLOTS = 16
LANES = 128
BLOCKS = 7
SHARE = BLOCKS * LANES
MEMBERS = 8
RING = 4
EXPERTS = 32
WIDTH = SHARE * MEMBERS
UNITS = 128
HEADS = 64
CTX = 1024
REQ = 2
GROUPS = 4
ROWS = 32
HALF = ROWS // 2
PLANES = 8
OFFSETS = (1, 7, 6, 3, 5, 4, 2, 0)
ACROSS = (2, 1, 3, 0)

SCALE = 0.07216878364870322
ROUTE_SCALE = 2.827
EPSILON = 1e-06
THETA = 50000.0
NEGATIVE = -1e30
LIFT = 2.0**60

ORDER = (
    ("S", 0), ("S", 1), ("S", 2), ("S", 3), ("P", 0), ("P", 1), ("E", 0), ("P", 2),
    ("E", 1), ("P", 3), ("E", 2), ("R", 0), ("E", 3), ("R", 1), ("R", 2), ("R", 3),
)

BF16 = jnp.bfloat16
F32 = jnp.float32
MESH = pl.DeviceIdType.MESH


def iota(shape, axis):
    return lax.broadcasted_iota(jnp.int32, shape, axis)


def kernel(
    counts_ref,
    lengths_ref,
    routes_hbm,
    gain_hbm,
    kv_gain_hbm,
    freq_hbm,
    drafts_hbm,
    cache_hbm,
    queries_hbm,
    kv_hbm,
    router_hbm,
    gate_hbm,
    up_hbm,
    down_hbm,
    drafted_ref,
    attended_ref,
    routes_ref,
    gain_ref,
    kv_gain_ref,
    freq_ref,
    cache,
    queries,
    kv,
    router,
    wgu,
    wd,
    start,
    x_ref,
    rgain,
    table,
    table_t,
    perm,
    a_out,
    a_in,
    rows_in,
    squares_ref,
    logits_ref,
    part_out,
    part_in,
    own_part,
    ring_out,
    ring_in,
    gates,
    d_out,
    d_in,
    lat_out,
    lat_in,
    keys,
    part_o,
    part_m,
    part_l,
    load_sem,
    wgu_sem,
    wd_sem,
    wgu_send,
    wd_send,
    a_send,
    a_recv,
    b_send,
    b_ring,
    p_send,
    p_recv,
    c_send,
    c_ring,
    d_send,
    d_recv,
    l_send,
    l_recv,
):
    dp = lax.axis_index("dp")
    ep = lax.axis_index("ep")
    z, xx = dp // RING, dp % RING
    y, core = ep // 2, ep % 2
    other = 1 - core
    sibling = 2 * y + other
    y_at = [(y + n) % RING for n in range(RING)]
    count = counts_ref[0]

    def load(src, dst, n):
        return pltpu.make_async_copy(src, dst, load_sem.at[n])

    router_base = pl.multiple_of((dp // 16) * 16, 16)
    loads = [
        load(routes_hbm, routes_ref, 0),
        load(drafts_hbm.at[:, pl.ds(pl.multiple_of(ep * SHARE, LANES), SHARE)], start, 1),
        load(gain_hbm, gain_ref, 2),
        load(kv_hbm, kv, 3),
        load(router_hbm.at[pl.ds(router_base, 16)], router, 4),
        load(kv_gain_hbm, kv_gain_ref, 5),
        load(freq_hbm, freq_ref, 6),
        load(cache_hbm, cache, 7),
        load(queries_hbm, queries, 8),
    ]
    for item in loads:
        item.start()

    def weight_views(side):
        views = []
        units = pl.ds(pl.multiple_of(core * UNITS, UNITS), UNITS)
        upper = pl.ds(pl.multiple_of((2 + core) * UNITS, UNITS), UNITS)
        for n in range(RING):
            features = pl.ds(pl.multiple_of((2 * n + side) * SHARE, LANES), SHARE)
            views.append((gate_hbm.at[0, features], wgu.at[n, :, units], wgu_sem, wgu_send))
            views.append((up_hbm.at[0, features], wgu.at[n, :, upper], wgu_sem, wgu_send))
        for n in range(RING):
            features = pl.ds(pl.multiple_of((2 * n + side) * SHARE, LANES), SHARE)
            views.append((down_hbm.at[0, :, features], wd.at[n, units], wd_sem, wd_send))
        return views

    for src, dst, sem, _ in weight_views(core):
        pltpu.make_async_copy(src, dst, sem).start()

    barrier = pltpu.get_barrier_semaphore()
    for n in range(1, EXPERTS):
        pl.semaphore_signal(
            barrier, inc=1, device_id=((dp + n) % EXPERTS, ep), device_id_type=MESH
        )
    for n in range(1, MEMBERS):
        pl.semaphore_signal(
            barrier, inc=1, device_id=(dp, (ep + n) % MEMBERS), device_id_type=MESH
        )

    pr = iota((32, LANES), 0)
    pc = iota((32, LANES), 1)
    pattern = jnp.where((pr >> 2) == (pc >> 4), pr & 3, -7).astype(F32)
    tri = jnp.where(iota((SLOTS, SLOTS), 0) < iota((SLOTS, SLOTS), 1), 1.0, 0.0).astype(BF16)
    spread = jnp.where(
        iota((SLOTS, LANES), 0) == (iota((SLOTS, LANES), 1) & 15), 1.0, 0.0
    ).astype(BF16)

    def build_table(s):
        expert = iota((EXPERTS, SLOTS), 0)
        live = iota((EXPERTS, SLOTS), 1) < count
        named = routes_ref[s]
        hit = expert == named[0:1, :]
        for k in range(1, TOP):
            hit = hit | (expert == named[k : k + 1, :])
        hit = hit & live
        before = jnp.dot(
            jnp.where(hit, 1.0, 0.0).astype(BF16), tri, preferred_element_type=F32
        )
        place = jnp.dot(
            jnp.where(hit, before, -1.0).astype(BF16), spread, preferred_element_type=F32
        )
        for e in range(EXPERTS):
            table[s, e * 32 : e * 32 + 32, :] = jnp.where(
                jnp.broadcast_to(place[e : e + 1, :], (32, LANES)) == pattern, 1.0, 0.0
            ).astype(BF16)

    def transpose_table(s):
        for n in range(8):
            table_t[s, :, n * LANES : (n + 1) * LANES] = (
                table[s, n * LANES : (n + 1) * LANES, :].astype(F32).T.astype(BF16)
            )

    def remote(src, dst, send, recv, device):
        pltpu.make_async_remote_copy(
            src_ref=src,
            dst_ref=dst,
            send_sem=send,
            recv_sem=recv,
            device_id=device,
            device_id_type=MESH,
        ).start()

    def arrive(ref, sem):
        pltpu.make_async_copy(ref, ref, sem).wait()

    def wait_slices(sem):
        arrive(rows_in.at[pl.ds(0, RING - 1), pl.ds(0, ROWS)], sem)

    def dispatch(s):
        xb = x_ref[...].astype(BF16)
        for i, dz in enumerate(OFFSETS):
            zt = (z + dz) % PLANES
            rows = table[s, pl.ds(pl.multiple_of(zt * LANES, LANES), LANES), :]
            picked = jnp.dot(rows, xb, preferred_element_type=F32).astype(BF16)
            a_out[pl.ds(zt * RING, RING)] = picked.reshape(RING, 32, LANES)
            for n, dx in enumerate(ACROSS):
                p = i * RING + n
                target = zt * RING + (xx + dx) % RING
                src, dst, sem = a_out.at[target], a_in.at[p], a_recv.at[p // PLANES]
                if dz == 0 and dx == 0:
                    pltpu.make_async_copy(src, dst, sem).start()
                else:
                    remote(src, dst, a_send, sem, (target, ep))

    def latent_send(s):
        parity = s % 2
        blocks = [x_ref[j * SLOTS : (j + 1) * SLOTS, :] for j in range(BLOCKS)]
        gained = [
            (blocks[j] * gain_ref[pl.ds(ep * BLOCKS + j, 1), :]).astype(BF16)
            for j in range(BLOCKS)
        ]
        latent = lax.dot_general(
            jnp.concatenate(gained, axis=1),
            kv[...],
            (((1,), (1,)), ((), ())),
            preferred_element_type=F32,
        )
        squares = blocks[0] * blocks[0]
        for j in range(1, BLOCKS):
            squares = squares + blocks[j] * blocks[j]
        squares = jnp.broadcast_to(jnp.sum(squares, axis=1, keepdims=True), (SLOTS, LANES))
        for t in range(SLOTS):
            row = (t % 2) * 8
            for jb in range(4):
                lat_out[t // 2, row + jb : row + jb + 1, :] = latent[
                    t : t + 1, jb * LANES : (jb + 1) * LANES
                ]
            lat_out[t // 2, row + 4 : row + 5, 0:64] = latent[t : t + 1, LAT:KD]
            lat_out[t // 2, row + 5 : row + 6, :] = squares[t : t + 1, :]
        for n in range(1, MEMBERS):
            target = (ep + n) % MEMBERS
            remote(
                lat_out.at[target], lat_in.at[parity, ep], l_send, l_recv.at[parity], (dp, target)
            )
        lat_in[parity, ep] = lat_out[ep]

    def latent_take(s):
        parity = s % 2
        arrive(lat_in.at[parity, pl.ds(0, MEMBERS - 1)], l_recv.at[parity])
        total = lat_in[parity, 0]
        for n in range(1, MEMBERS):
            total = total + lat_in[parity, n]
        scale = lax.rsqrt(total[5:6, :] * (1.0 / WIDTH) + EPSILON)
        scale_second = lax.rsqrt(total[13:14, :] * (1.0 / WIDTH) + EPSILON)
        raw = total * jnp.where(
            iota((16, LANES), 0) < 8,
            jnp.broadcast_to(scale, (16, LANES)),
            jnp.broadcast_to(scale_second, (16, LANES)),
        )
        position = jnp.where(
            iota((8, LANES), 0) == 0, lengths_ref[0] + s, lengths_ref[1] + s
        ).astype(F32)
        angle = position * freq_ref[...]
        cosine, sine = jnp.cos(angle), jnp.sin(angle)
        lane = iota((16, LANES), 1)
        ahead = jnp.where(lane < 32, -pltpu.roll(raw, LANES - 32, 1), 0.0)
        behind = jnp.where((lane >= 32) & (lane < 64), pltpu.roll(raw, 32, 1), 0.0)
        crossed = ahead + behind
        for q in range(REQ):
            base = q * 8
            lat = raw[base : base + 4, :]
            mean = jnp.sum(
                jnp.sum(lat * lat, axis=1, keepdims=True), axis=0, keepdims=True
            ) * (1.0 / LAT)
            lat = lat * lax.rsqrt(mean + EPSILON) * kv_gain_ref[...]
            for jb in range(4):
                keys[q, jb, pl.ds(s, 1), :] = lat[jb : jb + 1, :]
            keys[q, 4, pl.ds(s, 1), :] = (
                raw[base + 4 : base + 5, :] * cosine[q : q + 1, :]
                + crossed[base + 4 : base + 5, :] * sine[q : q + 1, :]
            )

    def attend_cache(q):
        query = queries[:, q].reshape(STEPS * HEADS, KD)
        score = SCALE * jnp.dot(query, cache[q], preferred_element_type=F32)
        valid = iota((STEPS * HEADS, CTX), 1) < lengths_ref[q]
        score = jnp.where(valid, score, NEGATIVE)
        top = jnp.max(score, axis=1, keepdims=True)
        prob = jnp.where(valid, jnp.exp(score - top), 0.0)
        part_m[q] = jnp.broadcast_to(top, (STEPS * HEADS, LANES))
        part_l[q] = jnp.broadcast_to(
            jnp.sum(prob, axis=1, keepdims=True), (STEPS * HEADS, LANES)
        )
        part_o[q] = lax.dot_general(
            prob.astype(BF16),
            cache[q, :LAT, :],
            (((1,), (1,)), ((), ())),
            preferred_element_type=F32,
        )

    def attend_draft(q):
        query = queries[:, q].reshape(STEPS * HEADS, KD)
        fresh = jnp.concatenate([keys[q, jb] for jb in range(5)], axis=1).astype(BF16)
        score = SCALE * lax.dot_general(
            query, fresh[:, :KD], (((1,), (1,)), ((), ())), preferred_element_type=F32
        )
        valid = iota((STEPS * HEADS, 8), 1) <= (iota((STEPS * HEADS, 8), 0) >> 6)
        score = jnp.where(valid, score, NEGATIVE)
        old_top = part_m[q][:, 0:1]
        top = jnp.maximum(jnp.max(score, axis=1, keepdims=True), old_top)
        prob = jnp.where(valid, jnp.exp(score - top), 0.0)
        shrink = jnp.exp(old_top - top)
        total = part_l[q][:, 0:1] * shrink + jnp.sum(prob, axis=1, keepdims=True)
        out = part_o[q] * shrink + jnp.dot(
            prob.astype(BF16), fresh[:, :LAT], preferred_element_type=F32
        )
        out = jnp.where((ep * REQ + q) < count, out / total, 0.0).astype(BF16)
        for n in range(STEPS):
            attended_ref[n, q] = out[n * HEADS : (n + 1) * HEADS, :]

    def absorb(g, at, first):
        e = 2 * at + core
        rows = slice(g * ROWS, (g + 1) * ROWS)
        gained = []
        for j in range(BLOCKS):
            wide = rows_in[at, rows, j * LANES : (j + 1) * LANES].astype(F32)
            gained.append((wide * gain_ref[pl.ds(e * BLOCKS + j, 1), :]).astype(BF16))
            square = wide * wide
            logit = wide * rgain[pl.ds(e * BLOCKS + j, 1), :]
            squares = square if j == 0 else squares + square
            logits = logit if j == 0 else logits + logit
        total = jnp.dot(
            jnp.concatenate(gained, axis=1), wgu[at], preferred_element_type=F32
        )
        if first:
            part_out[g, :, 0 : 4 * UNITS] = total
            squares_ref[g] = squares
            logits_ref[g] = logits
        else:
            part_out[g, :, 0 : 4 * UNITS] += total
            squares_ref[g] += squares
            logits_ref[g] += logits

    def gather_start(s, g):
        mates = pl.ds(g * PLANES, PLANES)
        arrive(a_in.at[mates], a_recv.at[g])
        block = a_in[mates].reshape(256, LANES)
        natural = jnp.dot(perm[...], block, preferred_element_type=F32).astype(BF16)
        rows = pl.ds(g * ROWS, ROWS)
        for j in range(BLOCKS):
            rows_in[y, rows, j * LANES : (j + 1) * LANES] = natural[j * ROWS : (j + 1) * ROWS, :]
        mine = rows_in.at[y, rows]
        for n in (2, 1, 3):
            remote(mine, mine, b_send.at[g], b_ring.at[g, n], (dp, 2 * y_at[n] + core))
        if g == 0:

            @pl.when(s == 0)
            def _():
                arrive(wgu, wgu_sem)

        absorb(g, y, True)

    def gather_pass(s, g):
        rows = pl.ds(g * ROWS, ROWS)
        for n in (1, 3, 2):
            at = y_at[RING - n]
            arrive(rows_in.at[at, rows], b_ring.at[g, n])
            absorb(g, at, False)
        lane = iota((ROWS, LANES), 1)
        part_out[g, :, 4 * UNITS :] = jnp.where(
            lane == 0,
            jnp.sum(squares_ref[g], axis=1, keepdims=True),
            jnp.where(lane == 1, jnp.sum(logits_ref[g], axis=1, keepdims=True), 0.0),
        )
        parity = s % 2
        remote(
            part_out.at[g], part_in.at[parity, g], p_send, p_recv.at[parity, g], (dp, sibling)
        )

    def expert(s, g):
        parity = s % 2
        arrive(part_in.at[parity, g], p_recv.at[parity, g])
        total = part_out[g] + part_in[parity, g]
        squares = total[:, 4 * UNITS : 4 * UNITS + 1]
        scale = lax.rsqrt(squares * (1.0 / WIDTH) + EPSILON)
        logit = total[:, 4 * UNITS + 1 : 4 * UNITS + 2] * scale
        gates[g] = jnp.broadcast_to(LIFT / (1.0 + jnp.exp(-logit)), (ROWS, LANES))
        first = total[:, : 2 * UNITS] * scale
        second = total[:, 2 * UNITS : 4 * UNITS] * scale
        hidden = (first / (1.0 + jnp.exp(-first)) * second).astype(BF16)
        if g == 0:

            @pl.when(s == 0)
            def _():
                arrive(wd, wd_sem)

        wait_slices(b_send.at[g])
        for n in (2, 1, 3):
            ring_out[g, n - 1] = jnp.dot(
                hidden, wd[y_at[n]], preferred_element_type=F32
            ).astype(BF16)
            remote(
                ring_out.at[g, n - 1],
                ring_in.at[g, n - 1],
                c_send.at[g],
                c_ring.at[g, n],
                (dp, 2 * y_at[n] + core),
            )
        own_part[g] = jnp.dot(hidden, wd[y], preferred_element_type=F32)

    def give_back(s, g):
        total = own_part[g]
        for n in (1, 3, 2):
            arrive(ring_in.at[g, n - 1], c_ring.at[g, n])
            total = total + ring_in[g, n - 1].astype(F32)
        gate = gates[g]
        parts = [
            (total[:, j * LANES : (j + 1) * LANES] * gate).astype(BF16) for j in range(BLOCKS)
        ]
        parts.append(gate.astype(BF16))
        block = jnp.dot(
            perm[...], jnp.concatenate(parts, axis=0), preferred_element_type=F32
        ).astype(BF16)

        d_out[pl.ds(g * PLANES, PLANES)] = block.reshape(PLANES, 32, LANES)
        for p in range(g * PLANES, (g + 1) * PLANES):
            dz, dx = OFFSETS[p // RING], ACROSS[p % RING]
            target = (z + PLANES - dz) % PLANES * RING + (xx + RING - dx) % RING
            if dz == 0 and dx == 0:
                pltpu.make_async_copy(d_out.at[p], d_in.at[dp], d_recv).start()
            else:
                remote(d_out.at[p], d_in.at[dp], d_send, d_recv, (target, ep))


    def combine(s):
        latent_take(s)

        @pl.when(s == STEPS - 1)
        def _():
            for q in range(REQ):
                attend_draft(q)

        arrive(d_in, d_recv)
        summed = jnp.dot(
            table_t[s], d_in[...].reshape(EXPERTS * 32, LANES), preferred_element_type=F32
        )
        weight = summed[BLOCKS * SLOTS :, :]
        alive = weight > 0.0
        factor = jnp.where(alive, ROUTE_SCALE / jnp.where(alive, weight, 1.0), 0.0)
        shown = iota((SLOTS, LANES), 0) < count
        for j in range(BLOCKS):
            rows = slice(j * SLOTS, (j + 1) * SLOTS)
            update = jnp.where(alive, summed[rows, :] * factor, 0.0)
            fresh = (x_ref[rows, :] + update).astype(BF16).astype(F32)
            x_ref[rows, :] = fresh
            drafted_ref[s, :, j * LANES : (j + 1) * LANES] = jnp.where(shown, fresh, 0.0).astype(
                BF16
            )
        arrive(a_out.at[pl.ds(0, EXPERTS - 1)], a_send)
        arrive(d_out.at[pl.ds(0, EXPERTS - 1)], d_send)
        arrive(lat_out.at[pl.ds(0, MEMBERS - 1)], l_send)

        @pl.when(s < STEPS - 1)
        def _():
            dispatch(s + 1)
            latent_send(s + 1)

        arrive(part_out, p_send)
        for g in range(GROUPS):
            wait_slices(c_send.at[g])

    loads[0].wait()
    build_table(0)
    lat_out[...] = jnp.zeros_like(lat_out)
    keys[...] = jnp.zeros_like(keys)
    loads[1].wait()
    for j in range(BLOCKS):
        x_ref[j * SLOTS : (j + 1) * SLOTS, :] = start[:, j * LANES : (j + 1) * LANES].astype(F32)
    x_ref[BLOCKS * SLOTS :, :] = jnp.zeros((SLOTS, LANES), F32)
    r = iota((256, 256), 0)
    c = iota((256, 256), 1)
    perm[...] = jnp.where(
        c == ((r >> 2) & 7) * 32 + (r >> 5) * 4 + (r & 3), 1.0, 0.0
    ).astype(BF16)
    pl.semaphore_wait(barrier, EXPERTS - 1 + MEMBERS - 1)
    for src, dst, sem, send in weight_views(other):
        remote(src, dst, send, sem, (dp, sibling))
    dispatch(0)
    loads[2].wait()
    loads[3].wait()
    latent_send(0)
    loads[4].wait()
    mine = iota((16, LANES), 0) == dp % 16
    for j in range(MEMBERS * BLOCKS):
        column = jnp.where(mine, router[:, j * LANES : (j + 1) * LANES].astype(F32), 0.0)
        rgain[j : j + 1, :] = jnp.sum(column, axis=0, keepdims=True) * gain_ref[j : j + 1, :]
    transpose_table(0)
    for n in range(1, STEPS):
        build_table(n)
        transpose_table(n)
    for n in range(5, 9):
        loads[n].wait()
    for q in range(REQ):
        attend_cache(q)

    events = {
        "S": gather_start,
        "P": gather_pass,
        "E": expert,
        "R": give_back,
    }

    def step(s, carry):
        for name, g in ORDER:
            events[name](s, g)
        combine(s)
        return carry

    lax.fori_loop(0, STEPS, step, 0)
    arrive(wgu.at[pl.ds(0, RING // 2)], wgu_send)
    arrive(wd.at[pl.ds(0, RING // 2)], wd_send)


def shards(
    drafts_in,
    cache,
    queries,
    lengths,
    counts,
    routes,
    norm_gain,
    kv_weight,
    kv_gain,
    router,
    w_gate,
    w_up,
    w_down,
):
    middle = (KD - LAT) // 2
    frequency = THETA ** (-np.arange(middle) / middle)
    frequency = np.concatenate([frequency, frequency, np.zeros(LANES - 2 * middle)])
    vmem = pl.BlockSpec(memory_space=pltpu.VMEM)
    smem = pl.BlockSpec(memory_space=pltpu.SMEM)
    hbm = pl.BlockSpec(memory_space=pltpu.HBM)
    dma = pltpu.SemaphoreType.DMA
    return pl.pallas_call(
        kernel,
        out_shape=(
            jax.ShapeDtypeStruct((STEPS, SLOTS, SHARE), BF16),
            jax.ShapeDtypeStruct((STEPS, REQ, HEADS, LAT), BF16),
        ),
        in_specs=[smem] * 2 + [hbm] * 12,
        out_specs=(vmem, vmem),
        scratch_shapes=[
            pltpu.VMEM((STEPS, TOP, SLOTS), jnp.int32),
            pltpu.VMEM((MEMBERS * BLOCKS, LANES), F32),
            pltpu.VMEM((LAT // LANES, LANES), F32),
            pltpu.VMEM((1, LANES), F32),
            pltpu.VMEM((REQ, KD, CTX), BF16),
            pltpu.VMEM((STEPS, REQ, HEADS, KD), BF16),
            pltpu.VMEM((KD, SHARE), BF16),
            pltpu.VMEM((16, WIDTH), BF16),
            pltpu.VMEM((RING, SHARE, 4 * UNITS), BF16),
            pltpu.VMEM((RING, 2 * UNITS, SHARE), BF16),
            pltpu.VMEM((SLOTS, SHARE), BF16),
            pltpu.VMEM((LANES, LANES), F32),
            pltpu.VMEM((MEMBERS * BLOCKS, LANES), F32),
            pltpu.VMEM((STEPS, EXPERTS * 32, LANES), BF16),
            pltpu.VMEM((STEPS, LANES, EXPERTS * 32), BF16),
            pltpu.VMEM((256, 256), BF16),
            pltpu.VMEM((EXPERTS, 32, LANES), BF16),
            pltpu.VMEM((EXPERTS, 32, LANES), BF16),
            pltpu.VMEM((RING, LANES, SHARE), BF16),
            pltpu.VMEM((GROUPS, ROWS, LANES), F32),
            pltpu.VMEM((GROUPS, ROWS, LANES), F32),
            pltpu.VMEM((GROUPS, ROWS, 5 * LANES), F32),
            pltpu.VMEM((2, GROUPS, ROWS, 5 * LANES), F32),
            pltpu.VMEM((GROUPS, ROWS, SHARE), F32),
            pltpu.VMEM((GROUPS, RING - 1, ROWS, SHARE), BF16),
            pltpu.VMEM((GROUPS, RING - 1, ROWS, SHARE), BF16),
            pltpu.VMEM((GROUPS, ROWS, LANES), F32),
            pltpu.VMEM((EXPERTS, 32, LANES), BF16),
            pltpu.VMEM((EXPERTS, 32, LANES), BF16),
            pltpu.VMEM((MEMBERS, 16, LANES), F32),
            pltpu.VMEM((2, MEMBERS, 16, LANES), F32),
            pltpu.VMEM((REQ, 5, 8, LANES), F32),
            pltpu.VMEM((REQ, STEPS * HEADS, LAT), F32),
            pltpu.VMEM((REQ, STEPS * HEADS, LANES), F32),
            pltpu.VMEM((REQ, STEPS * HEADS, LANES), F32),
            dma((9,)),
            dma,
            dma,
            dma,
            dma,
            dma,
            dma((GROUPS,)),
            dma((GROUPS,)),
            dma((GROUPS, RING)),
            dma,
            dma((2, GROUPS)),
            dma((GROUPS,)),
            dma((GROUPS, RING)),
            dma,
            dma,
            dma,
            dma((2,)),
        ],
        compiler_params=pltpu.CompilerParams(
            collective_id=0, has_side_effects=True, vmem_limit_bytes=60 * 1024 * 1024
        ),
        name="draft_steps",
    )(
        counts,
        lengths,
        jnp.swapaxes(routes, 1, 2),
        norm_gain.reshape(MEMBERS * BLOCKS, LANES),
        kv_gain.reshape(LAT // LANES, LANES),
        jnp.asarray(frequency[None, :], F32),
        drafts_in,
        jnp.swapaxes(cache, 1, 2),
        queries,
        jnp.swapaxes(kv_weight, 0, 1),
        jnp.swapaxes(router, 0, 1),
        w_gate,
        w_up,
        w_down,
    )


def solution(mesh):
    return jax.shard_map(
        shards,
        mesh=mesh,
        in_specs=(
            P("dp", None),
            P(("dp", "ep"), None, None),
            P(None, ("dp", "ep"), None, None),
            P(("dp", "ep")),
            P("dp"),
            P(None, "dp", None),
            P(),
            P("ep", None),
            P(),
            P(),
            P("dp", None, "ep"),
            P("dp", None, "ep"),
            P("dp", "ep", None),
        ),
        out_specs=(P(None, "dp", "ep"), P(None, ("dp", "ep"), None, None)),
        check_vma=False,
    )
```

time: 676 us -> 147 us (0.22); the launches traced: 664 us -> 146 us
  blocking collectives: 195 us -> 0 us
  waiting for transfers between devices: 186 us -> 0 us
  Pallas kernels: 0 us -> 142 us
  local copies, waits for them, and re-layouts: 124 us -> 3.42 us
  matrix products: 69.1 us -> 0 us
  starting transfers between devices: 45.8 us -> 0 us
  other arithmetic: 27.5 us -> 0 us
  between operations: 16.5 us -> 1.29 us
    all_to_all x3 -> x0, blocking collectives: 156 us -> none  [shards(): lax.all_to_all(outgoing, 'dp', split_axis=0, concat_axis=0, tiled=True)]
    unnamed x10 -> x0, waiting for transfers between devices: 151 us -> none
    pallas_call x0 -> x1, Pallas kernels: none -> 142 us  [shards(): pl.pallas_call(kernel, out_shape=(jax.ShapeDtypeStruct((STEPS, SLOTS, SHA...]
    unnamed x105 -> x2, local copies, waits for them, and re-layouts: 93.5 us -> 3.42 us
    dot_general x39 -> x0, matrix products: 69.1 us -> none  [the longest x4 19.7 us: shards(): jnp.einsum('sekf,efd->sekd', hidden_units, w_down, preferred_element_type...]
    all_to_all x5 -> x0, starting transfers between devices: 45.3 us -> none  [the longest x4 40.1 us: shards(): lax.all_to_all(summed, 'dp', split_axis=0, concat_axis=0, tiled=True)]
    all_gather x3 -> x0, blocking collectives: 38.5 us -> none  [shards(): hidden_state = lax.all_gather(new_slice, 'ep', axis=1, tiled=True)]
    all_to_all x5 -> x0, waiting for transfers between devices: 34.9 us -> none  [the longest x4 34.9 us: shards(): lax.all_to_all(summed, 'dp', split_axis=0, concat_axis=0, tiled=True)]
  transfers between devices with their start and end apart: 10 -> 0, of which waited for: 9 -> 0; matrix products, arithmetic and copies ran while one was open for 8% -> 0% of each run, Pallas kernels for 0% -> 0%
where the time goes in v2:
time: 147 us; the launch traced here: 146 us
  Pallas kernels  142 us (97%)
  local copies, waits for them, and re-layouts  3.42 us (2%)
    pallas_call x1, Pallas kernels, shards(): pl.pallas_call(kernel, out_shape=(jax.ShapeDtypeStruct((STEPS, SLOTS, SHA...  142 us
    unnamed x2, local copies, waits for them, and re-layouts  3.42 us

profile of v2, /device:TPU:32, one launch (start us, length us, event | category | flops | bytes accessed | tf_op | source)
XLA Modules:
  0.0 146.4 jit_solution(2477060414200511039)
XLA Ops:
  1.3 141.7 %draft_steps.1 = (bf16[4,16,896]{2,1,0:T(8,128)(2,1)}, bf16[4,2,64,512]{3,2,1,0:T(8,128)(2,1)}) custom-call(s32[1]{0:T(128)S(6)} %copy.18.counts_ref, s32[2]{0:T(128)} %lengths_ref.1, s32[4,8,16]{2,1,0:T(8,128)} %bitcast.10, f32[56,128]{1,0:T(8,128)} %bitcast.9, f32[4,128]{1,0:T(4,128)} %bitcast.11, f32[1,128]{1,0:T(1,128)} %constant.2.clone.freq_hbm, ...), custom_call_target="tpu_custom_call" | custom-call | tf_op jit(solution)/shard_map/draft_steps/pallas_call | solution.py:573
  143.0 1.6 %copy.19 = bf16[4,16,896]{2,1,0:T(8,128)(2,1)} copy(bf16[4,16,896]{2,1,0:T(8,128)(2,1)} %get-tuple-element.4) | data formatting | bytes 229376
  144.5 1.9 %copy.20 = bf16[4,2,64,512]{3,2,1,0:T(8,128)(2,1)} copy(bf16[4,2,64,512]{3,2,1,0:T(8,128)(2,1)} %get-tuple-element.5) | data formatting | bytes 1048576

commit v3 on v2

--- a/solution.py
+++ b/solution.py
@@ -23,12 +23,16 @@
 HEADS = 64
 CTX = 1024
 REQ = 2
-GROUPS = 4
-ROWS = 32
-HALF = ROWS // 2
 PLANES = 8
-OFFSETS = (1, 7, 6, 3, 5, 4, 2, 0)
+GROUPS = ((1, 7), (6, 3), (5, 4), (2,), (0,))
+DIRECT = (False, False, False, False, True)
+OFFSETS = tuple(dz for group in GROUPS for dz in group)
 ACROSS = (2, 1, 3, 0)
+RANKS = [4 * len(group) for group in GROUPS]
+FIRST = [sum(RANKS[:g]) for g in range(len(GROUPS))]
+ALONE = [g for g, direct in enumerate(DIRECT) if direct]
+GATHERED = sum(ranks for ranks, direct in zip(RANKS, DIRECT) if not direct)
+GROUP_OF = [g for g, ranks in enumerate(RANKS) for _ in range(ranks)]
 
 SCALE = 0.07216878364870322
 ROUTE_SCALE = 2.827
@@ -38,8 +42,7 @@
 LIFT = 2.0**60
 
 ORDER = (
-    ("S", 0), ("S", 1), ("S", 2), ("S", 3), ("P", 0), ("P", 1), ("E", 0), ("P", 2),
-    ("E", 1), ("P", 3), ("E", 2), ("R", 0), ("E", 3), ("R", 1), ("R", 2), ("R", 3),
+    ("S", 0), ("S", 1), ("S", 4), ("S", 2), ("P", 0), ("P", 4), ("S", 3), ("P", 1), ("E", 0), ("P", 2), ("E", 1), ("P", 3), ("E", 2), ("E", 3), ("E", 4), ("R", 0), ("R", 1), ("R", 2), ("R", 3),
 )
 
 BF16 = jnp.bfloat16
@@ -84,6 +87,8 @@
     table,
     table_t,
     perm,
+    perm_half,
+    perm_back,
     a_out,
     a_in,
     rows_in,
@@ -120,6 +125,7 @@
     d_recv,
     l_send,
     l_recv,
+    *direct_refs,
 ):
     dp = lax.axis_index("dp")
     ep = lax.axis_index("ep")
@@ -129,6 +135,8 @@
     sibling = 2 * y + other
     y_at = [(y + n) % RING for n in range(RING)]
     count = counts_ref[0]
+
+    near = {g: direct_refs[6 * n : 6 * n + 6] for n, g in enumerate(ALONE)}
 
     def load(src, dst, n):
         return pltpu.make_async_copy(src, dst, load_sem.at[n])
@@ -174,6 +182,17 @@
             barrier, inc=1, device_id=(dp, (ep + n) % MEMBERS), device_id_type=MESH
         )
 
+    around = [
+        ((z + dz) % PLANES * RING + (xx + dx) % RING, 2 * y_at[n] + core)
+        for g in ALONE
+        for dz in GROUPS[g]
+        for dx in range(RING)
+        for n in range(1, RING)
+        if dz != 0 or dx != 0
+    ]
+    for device in around:
+        pl.semaphore_signal(barrier, inc=1, device_id=device, device_id_type=MESH)
+
     pr = iota((32, LANES), 0)
     pc = iota((32, LANES), 1)
     pattern = jnp.where((pr >> 2) == (pc >> 4), pr & 3, -7).astype(F32)
@@ -220,8 +239,11 @@
     def arrive(ref, sem):
         pltpu.make_async_copy(ref, ref, sem).wait()
 
-    def wait_slices(sem):
-        arrive(rows_in.at[pl.ds(0, RING - 1), pl.ds(0, ROWS)], sem)
+    def span(g):
+        return pl.ds(FIRST[g] * CAP, RANKS[g] * CAP)
+
+    def wait_slices(g, sem):
+        arrive(rows_in.at[pl.ds(0, RING - 1), span(g)], sem.at[g])
 
     def dispatch(s):
         xb = x_ref[...].astype(BF16)
@@ -233,11 +255,18 @@
             for n, dx in enumerate(ACROSS):
                 p = i * RING + n
                 target = zt * RING + (xx + dx) % RING
-                src, dst, sem = a_out.at[target], a_in.at[p], a_recv.at[p // PLANES]
-                if dz == 0 and dx == 0:
-                    pltpu.make_async_copy(src, dst, sem).start()
-                else:
-                    remote(src, dst, a_send, sem, (target, ep))
+                g = GROUP_OF[p]
+                src, sem = a_out.at[target], a_recv.at[g]
+                if not DIRECT[g]:
+                    remote(src, a_in.at[p], a_send, sem, (target, ep))
+                    continue
+                rows_near, _, _, send, _, _ = near[g]
+                dst = rows_near.at[y * RANKS[g] + p - FIRST[g]]
+                for hop in (2, 1, 3, 0):
+                    if hop == 0 and dz == 0 and dx == 0:
+                        pltpu.make_async_copy(src, dst, sem).start()
+                    else:
+                        remote(src, dst, send, sem, (target, 2 * y_at[hop] + core))
 
     def latent_send(s):
         parity = s % 2
@@ -347,7 +376,7 @@
 
     def absorb(g, at, first):
         e = 2 * at + core
-        rows = slice(g * ROWS, (g + 1) * ROWS)
+        rows = span(g)
         gained = []
         for j in range(BLOCKS):
             wide = rows_in[at, rows, j * LANES : (j + 1) * LANES].astype(F32)
@@ -360,22 +389,38 @@
             jnp.concatenate(gained, axis=1), wgu[at], preferred_element_type=F32
         )
         if first:
-            part_out[g, :, 0 : 4 * UNITS] = total
-            squares_ref[g] = squares
-            logits_ref[g] = logits
+            part_out[rows, 0 : 4 * UNITS] = total
+            squares_ref[rows] = squares
+            logits_ref[rows] = logits
         else:
-            part_out[g, :, 0 : 4 * UNITS] += total
-            squares_ref[g] += squares
-            logits_ref[g] += logits
+            part_out[rows, 0 : 4 * UNITS] += total
+            squares_ref[rows] += squares
+            logits_ref[rows] += logits
 
     def gather_start(s, g):
-        mates = pl.ds(g * PLANES, PLANES)
+        ranks = RANKS[g]
+        rows, count_rows = span(g), ranks * CAP
+        turn = perm if ranks == 8 else perm_half
+
+        def settle(block, at):
+            natural = jnp.dot(
+                turn[...], block.reshape(ranks * 32, LANES), preferred_element_type=F32
+            ).astype(BF16)
+            for j in range(BLOCKS):
+                rows_in[at, rows, j * LANES : (j + 1) * LANES] = natural[
+                    j * count_rows : (j + 1) * count_rows, :
+                ]
+
+        if DIRECT[g]:
+            rows_near = near[g][0]
+            arrive(rows_near, a_recv.at[g])
+            for at in range(RING):
+                settle(rows_near[at * ranks : (at + 1) * ranks], at)
+                absorb(g, at, at == 0)
+            return
+        mates = pl.ds(FIRST[g], ranks)
         arrive(a_in.at[mates], a_recv.at[g])
-        block = a_in[mates].reshape(256, LANES)
-        natural = jnp.dot(perm[...], block, preferred_element_type=F32).astype(BF16)
-        rows = pl.ds(g * ROWS, ROWS)
-        for j in range(BLOCKS):
-            rows_in[y, rows, j * LANES : (j + 1) * LANES] = natural[j * ROWS : (j + 1) * ROWS, :]
+        settle(a_in[mates], y)
         mine = rows_in.at[y, rows]
         for n in (2, 1, 3):
             remote(mine, mine, b_send.at[g], b_ring.at[g, n], (dp, 2 * y_at[n] + core))
@@ -388,30 +433,31 @@
         absorb(g, y, True)
 
     def gather_pass(s, g):
-        rows = pl.ds(g * ROWS, ROWS)
-        for n in (1, 3, 2):
+        rows = span(g)
+        for n in () if DIRECT[g] else (1, 3, 2):
             at = y_at[RING - n]
             arrive(rows_in.at[at, rows], b_ring.at[g, n])
             absorb(g, at, False)
-        lane = iota((ROWS, LANES), 1)
-        part_out[g, :, 4 * UNITS :] = jnp.where(
+        lane = iota((RANKS[g] * CAP, LANES), 1)
+        part_out[rows, 4 * UNITS :] = jnp.where(
             lane == 0,
-            jnp.sum(squares_ref[g], axis=1, keepdims=True),
-            jnp.where(lane == 1, jnp.sum(logits_ref[g], axis=1, keepdims=True), 0.0),
+            jnp.sum(squares_ref[rows], axis=1, keepdims=True),
+            jnp.where(lane == 1, jnp.sum(logits_ref[rows], axis=1, keepdims=True), 0.0),
         )
         parity = s % 2
         remote(
-            part_out.at[g], part_in.at[parity, g], p_send, p_recv.at[parity, g], (dp, sibling)
+            part_out.at[rows], part_in.at[parity, rows], p_send, p_recv.at[parity, g], (dp, sibling)
         )
 
     def expert(s, g):
         parity = s % 2
-        arrive(part_in.at[parity, g], p_recv.at[parity, g])
-        total = part_out[g] + part_in[parity, g]
+        rows = span(g)
+        arrive(part_in.at[parity, rows], p_recv.at[parity, g])
+        total = part_out[rows] + part_in[parity, rows]
         squares = total[:, 4 * UNITS : 4 * UNITS + 1]
         scale = lax.rsqrt(squares * (1.0 / WIDTH) + EPSILON)
         logit = total[:, 4 * UNITS + 1 : 4 * UNITS + 2] * scale
-        gates[g] = jnp.broadcast_to(LIFT / (1.0 + jnp.exp(-logit)), (ROWS, LANES))
+        gates[rows] = jnp.broadcast_to(LIFT / (1.0 + jnp.exp(-logit)), (RANKS[g] * CAP, LANES))
         first = total[:, : 2 * UNITS] * scale
         second = total[:, 2 * UNITS : 4 * UNITS] * scale
         hidden = (first / (1.0 + jnp.exp(-first)) * second).astype(BF16)
@@ -421,43 +467,64 @@
             def _():
                 arrive(wd, wd_sem)
 
-        wait_slices(b_send.at[g])
+        if DIRECT[g]:
+            ranks = RANKS[g]
+            _, out, back, _, send, recv = near[g]
+            gate = gates[rows]
+            for n in (2, 1, 3, 0):
+                total = jnp.dot(hidden, wd[y_at[n]], preferred_element_type=F32)
+                fold(g, total, gate, gate * (1.0 / RING), out.at[pl.ds(n * ranks, ranks)])
+                for i in range(ranks):
+                    p = FIRST[g] + i
+                    target, own = home_of(p)
+                    src, dst = out.at[n * ranks + i], back.at[y * ranks + i]
+                    if own and n == 0:
+                        pltpu.make_async_copy(src, dst, recv).start()
+                    else:
+                        remote(src, dst, send, recv, (target, 2 * y_at[n] + core))
+            return
+        wait_slices(g, b_send)
         for n in (2, 1, 3):
-            ring_out[g, n - 1] = jnp.dot(
+            ring_out[n - 1, rows] = jnp.dot(
                 hidden, wd[y_at[n]], preferred_element_type=F32
             ).astype(BF16)
             remote(
-                ring_out.at[g, n - 1],
-                ring_in.at[g, n - 1],
+                ring_out.at[n - 1, rows],
+                ring_in.at[n - 1, rows],
                 c_send.at[g],
                 c_ring.at[g, n],
                 (dp, 2 * y_at[n] + core),
             )
-        own_part[g] = jnp.dot(hidden, wd[y], preferred_element_type=F32)
-
-    def give_back(s, g):
-        total = own_part[g]
-        for n in (1, 3, 2):
-            arrive(ring_in.at[g, n - 1], c_ring.at[g, n])
-            total = total + ring_in[g, n - 1].astype(F32)
-        gate = gates[g]
+        own_part[rows] = jnp.dot(hidden, wd[y], preferred_element_type=F32)
+
+    def home_of(p):
+        dz, dx = OFFSETS[p // RING], ACROSS[p % RING]
+        target = (z + PLANES - dz) % PLANES * RING + (xx + RING - dx) % RING
+        return target, dz == 0 and dx == 0
+
+    def fold(g, total, gate, share, out):
+        ranks = RANKS[g]
         parts = [
             (total[:, j * LANES : (j + 1) * LANES] * gate).astype(BF16) for j in range(BLOCKS)
         ]
-        parts.append(gate.astype(BF16))
+        parts.append(share.astype(BF16))
+        turn = perm if ranks == 8 else perm_back
         block = jnp.dot(
-            perm[...], jnp.concatenate(parts, axis=0), preferred_element_type=F32
+            turn[...], jnp.concatenate(parts, axis=0), preferred_element_type=F32
         ).astype(BF16)
-
-        d_out[pl.ds(g * PLANES, PLANES)] = block.reshape(PLANES, 32, LANES)
-        for p in range(g * PLANES, (g + 1) * PLANES):
-            dz, dx = OFFSETS[p // RING], ACROSS[p % RING]
-            target = (z + PLANES - dz) % PLANES * RING + (xx + RING - dx) % RING
-            if dz == 0 and dx == 0:
-                pltpu.make_async_copy(d_out.at[p], d_in.at[dp], d_recv).start()
-            else:
-                remote(d_out.at[p], d_in.at[dp], d_send, d_recv, (target, ep))
-
+        out[...] = block.reshape(ranks, 32, LANES)
+
+    def give_back(s, g):
+        rows = span(g)
+        total = own_part[rows]
+        for n in (1, 3, 2):
+            arrive(ring_in.at[n - 1, rows], c_ring.at[g, n])
+            total = total + ring_in[n - 1, rows].astype(F32)
+        gate = gates[rows]
+        fold(g, total, gate, gate, d_out.at[pl.ds(FIRST[g], RANKS[g])])
+        for p in range(FIRST[g], FIRST[g] + RANKS[g]):
+            target, _ = home_of(p)
+            remote(d_out.at[p], d_in.at[dp], d_send, d_recv, (target, ep))
 
     def combine(s):
         latent_take(s)
@@ -467,34 +534,50 @@
             for q in range(REQ):
                 attend_draft(q)
 
-        arrive(d_in, d_recv)
+        arrive(a_out.at[pl.ds(0, GATHERED)], a_send)
+        arrive(d_out.at[pl.ds(0, GATHERED)], d_send)
+        arrive(lat_out.at[pl.ds(0, MEMBERS - 1)], l_send)
+        arrive(part_out, p_send)
+        for g in range(len(GROUPS)):
+            if not DIRECT[g]:
+                wait_slices(g, c_send)
+        for g in ALONE:
+            ranks = RANKS[g]
+            rows_near, out, back, send, back_send, back_recv = near[g]
+            sent = pl.ds(0, RING * ranks - (1 if 0 in GROUPS[g] else 0))
+            arrive(rows_near.at[sent], send)
+            arrive(out.at[sent], back_send)
+            arrive(back, back_recv)
+            for i in range(ranks):
+                p = FIRST[g] + i
+                dz, dx = OFFSETS[p // RING], ACROSS[p % RING]
+                block = back[i].astype(F32)
+                for n in range(1, RING):
+                    block = block + back[n * ranks + i].astype(F32)
+                d_in[(z + dz) % PLANES * RING + (xx + dx) % RING] = block.astype(BF16)
+        arrive(d_in.at[pl.ds(0, GATHERED)], d_recv)
         summed = jnp.dot(
             table_t[s], d_in[...].reshape(EXPERTS * 32, LANES), preferred_element_type=F32
         )
         weight = summed[BLOCKS * SLOTS :, :]
         alive = weight > 0.0
         factor = jnp.where(alive, ROUTE_SCALE / jnp.where(alive, weight, 1.0), 0.0)
-        shown = iota((SLOTS, LANES), 0) < count
         for j in range(BLOCKS):
             rows = slice(j * SLOTS, (j + 1) * SLOTS)
             update = jnp.where(alive, summed[rows, :] * factor, 0.0)
-            fresh = (x_ref[rows, :] + update).astype(BF16).astype(F32)
-            x_ref[rows, :] = fresh
-            drafted_ref[s, :, j * LANES : (j + 1) * LANES] = jnp.where(shown, fresh, 0.0).astype(
-                BF16
-            )
-        arrive(a_out.at[pl.ds(0, EXPERTS - 1)], a_send)
-        arrive(d_out.at[pl.ds(0, EXPERTS - 1)], d_send)
-        arrive(lat_out.at[pl.ds(0, MEMBERS - 1)], l_send)
+            x_ref[rows, :] = (x_ref[rows, :] + update).astype(BF16).astype(F32)
 
         @pl.when(s < STEPS - 1)
         def _():
             dispatch(s + 1)
             latent_send(s + 1)
 
-        arrive(part_out, p_send)
-        for g in range(GROUPS):
-            wait_slices(c_send.at[g])
+        shown = iota((SLOTS, LANES), 0) < count
+        for j in range(BLOCKS):
+            fresh = x_ref[j * SLOTS : (j + 1) * SLOTS, :]
+            drafted_ref[s, :, j * LANES : (j + 1) * LANES] = jnp.where(shown, fresh, 0.0).astype(
+                BF16
+            )
 
     loads[0].wait()
     build_table(0)
@@ -509,7 +592,15 @@
     perm[...] = jnp.where(
         c == ((r >> 2) & 7) * 32 + (r >> 5) * 4 + (r & 3), 1.0, 0.0
     ).astype(BF16)
-    pl.semaphore_wait(barrier, EXPERTS - 1 + MEMBERS - 1)
+    r = iota((LANES, LANES), 0)
+    c = iota((LANES, LANES), 1)
+    perm_half[...] = jnp.where(
+        c == ((r >> 2) & 3) * 32 + (r >> 4) * 4 + (r & 3), 1.0, 0.0
+    ).astype(BF16)
+    perm_back[...] = jnp.where(
+        r == ((c >> 2) & 3) * 32 + (c >> 4) * 4 + (c & 3), 1.0, 0.0
+    ).astype(BF16)
+    pl.semaphore_wait(barrier, EXPERTS - 1 + MEMBERS - 1 + len(around))
     for src, dst, sem, send in weight_views(other):
         remote(src, dst, send, sem, (dp, sibling))
     dispatch(0)
@@ -546,6 +637,19 @@
     lax.fori_loop(0, STEPS, step, 0)
     arrive(wgu.at[pl.ds(0, RING // 2)], wgu_send)
     arrive(wd.at[pl.ds(0, RING // 2)], wd_send)
+
+
+def hand_over(drafted_in, attended_in, drafted_out, attended_out, *held):
+    pairs = ((attended_in, held[0], attended_out), (drafted_in, held[1], drafted_out))
+    into = [pltpu.make_async_copy(a, b, held[2].at[n]) for n, (a, b, _) in enumerate(pairs)]
+    back = [pltpu.make_async_copy(b, c, held[3].at[n]) for n, (_, b, c) in enumerate(pairs)]
+    for item in into:
+        item.start()
+    for first, second in zip(into, back):
+        first.wait()
+        second.start()
+    for item in back:
+        item.wait()
 
 
 def shards(
@@ -570,7 +674,7 @@
     smem = pl.BlockSpec(memory_space=pltpu.SMEM)
     hbm = pl.BlockSpec(memory_space=pltpu.HBM)
     dma = pltpu.SemaphoreType.DMA
-    return pl.pallas_call(
+    results = pl.pallas_call(
         kernel,
         out_shape=(
             jax.ShapeDtypeStruct((STEPS, SLOTS, SHARE), BF16),
@@ -595,17 +699,19 @@
             pltpu.VMEM((STEPS, EXPERTS * 32, LANES), BF16),
             pltpu.VMEM((STEPS, LANES, EXPERTS * 32), BF16),
             pltpu.VMEM((256, 256), BF16),
+            pltpu.VMEM((LANES, LANES), BF16),
+            pltpu.VMEM((LANES, LANES), BF16),
             pltpu.VMEM((EXPERTS, 32, LANES), BF16),
             pltpu.VMEM((EXPERTS, 32, LANES), BF16),
             pltpu.VMEM((RING, LANES, SHARE), BF16),
-            pltpu.VMEM((GROUPS, ROWS, LANES), F32),
-            pltpu.VMEM((GROUPS, ROWS, LANES), F32),
-            pltpu.VMEM((GROUPS, ROWS, 5 * LANES), F32),
-            pltpu.VMEM((2, GROUPS, ROWS, 5 * LANES), F32),
-            pltpu.VMEM((GROUPS, ROWS, SHARE), F32),
-            pltpu.VMEM((GROUPS, RING - 1, ROWS, SHARE), BF16),
-            pltpu.VMEM((GROUPS, RING - 1, ROWS, SHARE), BF16),
-            pltpu.VMEM((GROUPS, ROWS, LANES), F32),
+            pltpu.VMEM((LANES, LANES), F32),
+            pltpu.VMEM((LANES, LANES), F32),
+            pltpu.VMEM((LANES, 5 * LANES), F32),
+            pltpu.VMEM((2, LANES, 5 * LANES), F32),
+            pltpu.VMEM((LANES, SHARE), F32),
+            pltpu.VMEM((RING - 1, LANES, SHARE), BF16),
+            pltpu.VMEM((RING - 1, LANES, SHARE), BF16),
+            pltpu.VMEM((LANES, LANES), F32),
             pltpu.VMEM((EXPERTS, 32, LANES), BF16),
             pltpu.VMEM((EXPERTS, 32, LANES), BF16),
             pltpu.VMEM((MEMBERS, 16, LANES), F32),
@@ -620,17 +726,29 @@
             dma,
             dma,
             dma,
-            dma((GROUPS,)),
-            dma((GROUPS,)),
-            dma((GROUPS, RING)),
+            dma((len(GROUPS),)),
+            dma((len(GROUPS),)),
+            dma((len(GROUPS), RING)),
             dma,
-            dma((2, GROUPS)),
-            dma((GROUPS,)),
-            dma((GROUPS, RING)),
+            dma((2, len(GROUPS))),
+            dma((len(GROUPS),)),
+            dma((len(GROUPS), RING)),
             dma,
             dma,
             dma,
             dma((2,)),
+            *[
+                ref
+                for g in ALONE
+                for ref in (
+                    pltpu.VMEM((RING * RANKS[g], 32, LANES), BF16),
+                    pltpu.VMEM((RING * RANKS[g], 32, LANES), BF16),
+                    pltpu.VMEM((RING * RANKS[g], 32, LANES), BF16),
+                    dma,
+                    dma,
+                    dma,
+                )
+            ],
         ],
         compiler_params=pltpu.CompilerParams(
             collective_id=0, has_side_effects=True, vmem_limit_bytes=60 * 1024 * 1024
@@ -652,6 +770,19 @@
         w_up,
         w_down,
     )
+    return pl.pallas_call(
+        hand_over,
+        out_shape=tuple(jax.ShapeDtypeStruct(r.shape, r.dtype) for r in results),
+        in_specs=[hbm, hbm],
+        out_specs=(hbm, hbm),
+        scratch_shapes=[
+            pltpu.VMEM(results[1].shape, BF16),
+            pltpu.VMEM(results[0].shape, BF16),
+            dma((2,)),
+            dma((2,)),
+        ],
+        name="hand_over",
+    )(*results)
 
 
 def solution(mesh):

time: 147 us -> 145 us (0.986)
  local copies, waits for them, and re-layouts: 3.42 us -> 0 us
    unnamed x2 -> x0, local copies, waits for them, and re-layouts: 3.42 us -> none
    pallas_call x0 -> x1, Pallas kernels: none -> 1.89 us  [shards(): pl.pallas_call(hand_over, out_shape=tuple((jax.ShapeDtypeStruct(r.shape,...]
    pallas_call x1, Pallas kernels: 142 us -> 140 us  [shards(): pl.pallas_call(kernel, out_shape=(jax.ShapeDtypeStruct((STEPS, SLOTS, SHA...]
where the time goes in v3:
time: 145 us; the launch traced here: 143 us
  Pallas kernels  142 us (98%)
    pallas_call x1, Pallas kernels, shards(): pl.pallas_call(kernel, out_shape=(jax.ShapeDtypeStruct((STEPS, SLOTS, SHA...  140 us

profile of v3, /device:TPU:32, one launch (start us, length us, event | category | flops | bytes accessed | tf_op | source)
XLA Modules:
  0.0 143.4 jit_solution(2298871431775672968)
XLA Ops:
  1.3 140.2 %draft_steps.1 = (bf16[4,16,896]{2,1,0:T(8,128)(2,1)}, bf16[4,2,64,512]{3,2,1,0:T(8,128)(2,1)}) custom-call(s32[1]{0:T(128)S(6)} %copy.16.counts_ref, s32[2]{0:T(128)} %lengths_ref.1, s32[4,8,16]{2,1,0:T(8,128)} %bitcast.10, f32[56,128]{1,0:T(8,128)} %bitcast.9, f32[4,128]{1,0:T(4,128)} %bitcast.11, f32[1,128]{1,0:T(1,128)} %constant.2.clone.freq_hbm, ...), custom_call_target="tpu_custom_call" | custom-call | tf_op jit(solution)/shard_map/draft_steps/pallas_call | solution.py:677
  141.5 1.9 %hand_over.1 = (bf16[4,16,896]{2,1,0:T(8,128)(2,1)}, bf16[4,2,64,512]{3,2,1,0:T(8,128)(2,1)}) custom-call(bf16[4,16,896]{2,1,0:T(8,128)(2,1)} %get-tuple-element.4.drafted_in, bf16[4,2,64,512]{3,2,1,0:T(8,128)(2,1)} %get-tuple-element.5.attended_in), custom_call_target="tpu_custom_call" | custom-call | tf_op jit(solution)/shard_map/hand_over/pallas_call | solution.py:773

commit v4 on v3

--- a/solution.py
+++ b/solution.py
@@ -42,7 +42,7 @@
 LIFT = 2.0**60
 
 ORDER = (
-    ("S", 0), ("S", 1), ("S", 4), ("S", 2), ("P", 0), ("P", 4), ("S", 3), ("P", 1), ("E", 0), ("P", 2), ("E", 1), ("P", 3), ("E", 2), ("E", 3), ("E", 4), ("R", 0), ("R", 1), ("R", 2), ("R", 3),
+    ("S", 0), ("S", 1), ("S", 2), ("S", 3), ("P", 0), ("S", 4), ("P", 4), ("P", 1), ("E", 0), ("P", 2), ("E", 1), ("P", 3), ("E", 2), ("E", 3), ("R", 0), ("E", 4), ("R", 1), ("R", 2), ("R", 3),
 )
 
 BF16 = jnp.bfloat16

time: 145 us -> 144 us (level)
  no operation moved by 1% of the time
where the time goes in v4:
time: 144 us; the launch traced here: 143 us
  Pallas kernels  142 us (99%)
    pallas_call x1, Pallas kernels, shards(): pl.pallas_call(kernel, out_shape=(jax.ShapeDtypeStruct((STEPS, SLOTS, SHA...  140 us

profile of v4, /device:TPU:32, one launch (start us, length us, event | category | flops | bytes accessed | tf_op | source)
XLA Modules:
  0.0 142.8 jit_solution(11841311785285231478)
XLA Ops:
  1.3 139.6 %draft_steps.1 = (bf16[4,16,896]{2,1,0:T(8,128)(2,1)}, bf16[4,2,64,512]{3,2,1,0:T(8,128)(2,1)}) custom-call(s32[1]{0:T(128)S(6)} %copy.16.counts_ref, s32[2]{0:T(128)} %lengths_ref.1, s32[4,8,16]{2,1,0:T(8,128)} %bitcast.10, f32[56,128]{1,0:T(8,128)} %bitcast.9, f32[4,128]{1,0:T(4,128)} %bitcast.11, f32[1,128]{1,0:T(1,128)} %constant.2.clone.freq_hbm, ...), custom_call_target="tpu_custom_call" | custom-call | tf_op jit(solution)/shard_map/draft_steps/pallas_call | solution.py:677
  140.9 1.9 %hand_over.1 = (bf16[4,16,896]{2,1,0:T(8,128)(2,1)}, bf16[4,2,64,512]{3,2,1,0:T(8,128)(2,1)}) custom-call(bf16[4,16,896]{2,1,0:T(8,128)(2,1)} %get-tuple-element.4.drafted_in, bf16[4,2,64,512]{3,2,1,0:T(8,128)(2,1)} %get-tuple-element.5.attended_in), custom_call_target="tpu_custom_call" | custom-call | tf_op jit(solution)/shard_map/hand_over/pallas_call | solution.py:773
